TPU v7x, 512 devices: a whole 4x4x16 slice. The times are simulated.
512 devices in a mesh: inst: 64 (over y_lo, z, core), tp: 8 (over x, y_hi).
Axes of the slice: x: 4, y: 4 (y_hi: 2, y_lo: 2; y = y_hi * 2 + y_lo), z: 16, core: 2. Of those that a mesh axis runs over, the one named last changes fastest.
Arguments:
- hidden_state: bfloat16 [8192, 6144], P('inst', 'tp'), may hold values from -3000 to 3000
- norm_gain: bfloat16 [6144], P('tp'), may hold values from 0.099609375 to 1.8984375
- kv_weight: bfloat16 [6144, 8, 256], P('tp'), may hold values from -0.078125 to 0.078125
- queries: bfloat16 [8192, 48, 128], P('inst', 'tp'), may hold values from -120 to 120
- pool_keys: bfloat16 [1280, 8, 128, 128], P('inst', 'tp'), may hold values from -6 to 6
- pool_values: bfloat16 [1280, 8, 128, 128], P('inst', 'tp'), may hold values from -6 to 6
- page_table: int32 [8192, 12], P('inst'), may hold values from 0 to 19, as said below
- lengths: int32 [8192], P('inst'), may hold values from 2 to 1536
- move_target: int32 [2048, 1], P('inst'), may hold values from 0 to 63; in each aligned block of 32 rows (0 to 31, 32 to 63, ...) no two rows name the same one
- move_page: int32 [2048], P('inst'), may hold values from 0 to 19
- move_request: int32 [2048], P('inst'), may hold values from 0 to 127
Outputs:
- attention_out: bfloat16 [8192, 6144], P('inst', 'tp')
- new_kv: bfloat16 [8192, 8, 256], P('inst', 'tp')
Inputs may be any that keep to these rules, and one draw needn't show every extreme that they name: `page_table`: each row names 12 distinct pages of its instance's pool. `move_target`: the 32 rows of one instance never name the same destination twice.
All inputs are finite; a program needn't handle non-finite values.
Results may differ from a plain program's by a relative error of at most 0.005.
Values may be sent and summed in bfloat16 or wider, within the bound.
No kernel may reach another device: no remote copies, remote signals or barrier semaphores. Data moves between devices by JAX's collectives and lax.ppermute only.
A program may use at most 64 MiB of HBM per device.

v0:
```python
import math

import jax
import jax.numpy as jnp
from jax import lax
from jax.sharding import PartitionSpec as P

EPSILON = 1e-05
ROPE_BASE = 1000000.0
FLOOR_SCORE = -1e30


def rotate_keys(key_rows, positions):
    half_width = key_rows.shape[-1] // 2
    freq_steps = jnp.arange(half_width, dtype=jnp.float32)
    frequency = ROPE_BASE ** (-2.0 * freq_steps / key_rows.shape[-1])
    angles = positions.astype(jnp.float32)[:, None, None] * frequency[None, None, :]
    first_half = key_rows[..., :half_width]
    second_half = key_rows[..., half_width:]
    cosine = jnp.cos(angles)
    sine_part = jnp.sin(angles)
    return jnp.concatenate(
        [
            first_half * cosine - second_half * sine_part,
            second_half * cosine + first_half * sine_part,
        ],
        axis=-1,
    )


def page_blocks(query_rows, key_pages, value_pages, scaling):
    scores = (
        jnp.einsum("ngqd,ngtd->ngqt", query_rows, key_pages, preferred_element_type=jnp.float32)
        * scaling
    )
    highest = jnp.max(scores, axis=-1)
    weights = jnp.exp(scores - highest[..., None])
    block_sum = jnp.sum(weights, axis=-1)
    block_out = jnp.einsum(
        "ngqt,ngtd->ngqd",
        weights.astype(jnp.bfloat16),
        value_pages,
        preferred_element_type=jnp.float32,
    )
    return (highest, block_sum, block_out)


def body(
    hidden_state,
    norm_gain,
    kv_weight,
    queries,
    pool_keys,
    pool_values,
    page_table,
    lengths,
    move_target,
    move_page,
    move_request,
):
    widened = hidden_state.astype(jnp.float32)
    squares = lax.psum(jnp.sum(widened * widened, axis=1), "tp")
    features = hidden_state.shape[1] * lax.axis_size("tp")
    inverse = lax.rsqrt(squares / features + EPSILON)
    normed = (widened * inverse[:, None] * norm_gain.astype(jnp.float32)[None, :]).astype(
        jnp.bfloat16
    )
    projected = jnp.transpose(
        lax.psum_scatter(
            jnp.einsum("rf,fgc->grc", normed, kv_weight, preferred_element_type=jnp.float32),
            "tp",
            scatter_dimension=0,
            tiled=True,
        ),
        (1, 0, 2),
    )
    requests, query_heads, head_dim = queries.shape
    rotated = rotate_keys(projected[:, :, :head_dim], lengths)
    new_kv = jnp.concatenate([rotated, projected[:, :, head_dim:]], axis=-1).astype(jnp.bfloat16)
    pool_size, key_heads, page_len = (pool_keys.shape[0], pool_keys.shape[1], pool_keys.shape[2])
    group_size = query_heads // key_heads
    scaling = 1.0 / math.sqrt(head_dim)
    grouped = queries.reshape(requests, key_heads, group_size, head_dim)
    scores = (
        jnp.einsum("rgqd,pgtd->rgqpt", grouped, pool_keys, preferred_element_type=jnp.float32)
        * scaling
    )
    matches = page_table[:, :, None] == jnp.arange(pool_size, dtype=jnp.int32)[None, None, :]
    slot_of = jnp.sum(
        jnp.where(matches, jnp.arange(page_table.shape[1], dtype=jnp.int32)[None, :, None], 0),
        axis=1,
    )
    present = jnp.any(matches, axis=1)
    token_pos = (
        slot_of[:, :, None] * page_len + jnp.arange(page_len, dtype=jnp.int32)[None, None, :]
    )
    usable = (present[:, :, None] & (token_pos < lengths[:, None, None]))[:, None, None]
    masked = jnp.where(usable, scores, FLOOR_SCORE)
    local_high = jnp.max(masked, axis=-1)
    local_weights = jnp.where(usable, jnp.exp(masked - local_high[..., None]), 0.0)
    local_sums = jnp.sum(local_weights, axis=-1)
    local_out = jnp.einsum(
        "rgqpt,pgtd->rgqpd",
        local_weights.astype(jnp.bfloat16),
        pool_values,
        preferred_element_type=jnp.float32,
    )
    fresh_key = new_kv[:, :, :head_dim]
    fresh_value = new_kv[:, :, head_dim:].astype(jnp.float32)
    fresh_score = (
        jnp.einsum("rgqd,rgd->rgq", grouped, fresh_key, preferred_element_type=jnp.float32)
        * scaling
    )
    instances = lax.axis_size("inst")
    targets = move_target[:, 0]
    chosen = targets[None, :] == jnp.arange(instances, dtype=jnp.int32)[:, None]
    filled = jnp.any(chosen, axis=1)
    source_page = jnp.sum(jnp.where(chosen, move_page[None, :], 0), axis=1)
    label_out = jnp.where(filled, jnp.sum(jnp.where(chosen, move_request[None, :], 0), axis=1), -1)
    recv_keys, recv_values, labels_in = (
        lax.all_to_all(pool_keys[source_page], "inst", split_axis=0, concat_axis=0, tiled=True),
        lax.all_to_all(pool_values[source_page], "inst", split_axis=0, concat_axis=0, tiled=True),
        lax.all_to_all(label_out, "inst", split_axis=0, concat_axis=0, tiled=True),
    )
    asked_rows = grouped[jnp.maximum(labels_in, 0)]
    moved_high, moved_sums, moved_out = page_blocks(asked_rows, recv_keys, recv_values, scaling)
    valid_in = labels_in >= 0
    owners = labels_in[None, :] == jnp.arange(requests, dtype=jnp.int32)[:, None]
    moved_best = jnp.max(jnp.where(owners[:, :, None, None], moved_high[None], FLOOR_SCORE), axis=1)
    row_best = jnp.maximum(jnp.maximum(jnp.max(local_high, axis=-1), fresh_score), moved_best)
    local_factor = jnp.exp(local_high - row_best[..., None])
    fresh_factor = jnp.exp(fresh_score - row_best)
    moved_factor = jnp.where(
        valid_in[:, None, None], jnp.exp(moved_high - row_best[jnp.maximum(labels_in, 0)]), 0.0
    )
    owner_matrix = owners.astype(jnp.float32)
    denominator = (
        jnp.sum(local_factor * local_sums, axis=-1)
        + fresh_factor
        + jnp.einsum(
            "rn,ngq->rgq", owner_matrix, moved_factor * moved_sums, precision=lax.Precision.HIGHEST
        )
    )
    numerator = (
        jnp.sum(local_factor[..., None] * local_out, axis=3)
        + fresh_factor[..., None] * fresh_value[:, :, None, :]
    )
    numerator = numerator + jnp.einsum(
        "rn,ngqd->rgqd",
        owner_matrix,
        moved_factor[..., None] * moved_out,
        precision=lax.Precision.HIGHEST,
    )
    attention_out = (
        (numerator / denominator[..., None])
        .astype(jnp.bfloat16)
        .reshape(requests, query_heads * head_dim)
    )
    return (attention_out, new_kv)


def solution(mesh):
    return jax.shard_map(
        body,
        mesh=mesh,
        in_specs=(
            P("inst", "tp"),
            P("tp"),
            P("tp", None, None),
            P("inst", "tp", None),
            P("inst", "tp", None, None),
            P("inst", "tp", None, None),
            P("inst", None),
            P("inst"),
            P("inst", None),
            P("inst"),
            P("inst"),
        ),
        out_specs=(P("inst", "tp"), P("inst", "tp", None)),
        check_vma=False,
    )
```

profile of v0, /device:TPU:1, one launch (start us, length us, event | category | flops | bytes accessed | tf_op | source)
XLA Modules:
  0.0 292.7 jit_solution(2780683304075647802)
XLA Ops:
  7.2 0.9 fusion.66
  8.1 0.8 select_reduce_fusion.3
  8.9 0.7 copy.54
  9.6 18.2 %all-to-all-start = ((s32[64,1,1]{2,1,0:T(1,128)}), s32[64,1,1]{2,1,0:T(1,128)S(1)}, u32[]{:S(2)}, u32[]{:S(2)}) async-start(s32[64,1,1]{2,1,0:T(1,128)} %copy.54), calls=%async_computation.1 | async-start | bytes 65536 | tf_op jit(solution)/shard_map/all_to_all | solution.py:123
  27.8 3.2 %gather_fusion.1 = bf16[64,128,128]{2,1,0:T(8,128)(2,1)} fusion(bf16[20,128,128]{2,1,0:T(8,128)(2,1)} %bitcast.93, s32[1024]{0:T(1024)S(1)} %pad_clamp_fusion), kind=kCustom, calls=%fused_computation.1 | custom fusion | bytes 4194560 | tf_op jit(solution)/shard_map/gather | solution.py:121
  31.1 9.9 %all-to-all-done = s32[64,1,1]{2,1,0:T(1,128)S(1)} async-done(((s32[64,1,1]{2,1,0:T(1,128)}), s32[64,1,1]{2,1,0:T(1,128)S(1)}, u32[]{:S(2)}, u32[]{:S(2)}) %all-to-all-start) | async-done | bytes 288 | tf_op jit(solution)/shard_map/all_to_all | solution.py:123
  41.0 5.5 %all-to-all-start.1 = ((bf16[64,1,128,128]{3,2,1,0:T(8,128)(2,1)}), bf16[64,1,128,128]{3,2,1,0:T(8,128)(2,1)}, u32[]{:S(2)}, u32[]{:S(2)}) async-start(bf16[64,1,128,128]{3,2,1,0:T(8,128)(2,1)} %bitcast.95), calls=%async_computation.2 | async-start | bytes 4194304 | tf_op jit(solution)/shard_map/all_to_all | solution.py:121
  46.5 3.3 %gather_fusion.3 = bf16[64,128,128]{2,1,0:T(8,128)(2,1)} fusion(bf16[20,128,128]{2,1,0:T(8,128)(2,1)} %bitcast.96, s32[1024]{0:T(1024)S(1)} %pad_clamp_fusion), kind=kCustom, calls=%fused_computation.3 | custom fusion | bytes 4194560 | tf_op jit(solution)/shard_map/gather | solution.py:122
  49.9 92.0 %all-to-all-done.1 = bf16[64,1,128,128]{3,2,1,0:T(8,128)(2,1)} async-done(((bf16[64,1,128,128]{3,2,1,0:T(8,128)(2,1)}), bf16[64,1,128,128]{3,2,1,0:T(8,128)(2,1)}, u32[]{:S(2)}, u32[]{:S(2)}) %all-to-all-start.1) | async-done | bytes 2097184 | tf_op jit(solution)/shard_map/all_to_all | solution.py:121
  141.8 9.8 %all-to-all-start.2 = ((bf16[64,1,128,128]{3,2,1,0:T(8,128)(2,1)}), bf16[64,1,128,128]{3,2,1,0:T(8,128)(2,1)}, u32[]{:S(2)}, u32[]{:S(2)}) async-start(bf16[64,1,128,128]{3,2,1,0:T(8,128)(2,1)} %bitcast.94), calls=%async_computation.3 | async-start | bytes 4194304 | tf_op jit(solution)/shard_map/all_to_all | solution.py:122
  151.7 1.0 fusion.36
  152.8 21.3 %psum.7 = f32[128]{0:T(128)S(1)} all-reduce(f32[128]{0:T(128)S(1)} %fusion.36), channel_id=1, replica_groups=mesh['inst'=64,'tp'=8] {'tp'}, use_global_device_ids=true, to_apply=%region_5.6 | all-reduce | flops 128 | bytes 1024 | tf_op jit(solution)/shard_map/psum | solution.py:62
  174.1 2.6 fusion.21
  177.1 2.6 fusion.4
  179.7 3.1 %copy-done.1 = f32[20,128,128,6]{2,1,3,0:T(8,128)} copy-done((f32[20,128,128,6]{2,1,3,0:T(8,128)}, f32[20,128,128,6]{2,1,3,0:T(8,128)S(1)}, u32[]{:S(2)}) %copy-start.1) | copy-done | bytes 7864344
  182.8 3.3 %fusion.1 = (f32[128,6,20]{0,1,2:T(8,128)}, f32[128,6]{0,1:T(8,128)S(1)}) fusion(f32[20,128,128,6]{2,1,3,0:T(8,128)S(1)} %get-tuple-element.27, f32[128,6,20]{0,1,2:T(8,128)S(1)} %get-tuple-element.26, pred[128,20,128]{0,2,1:T(8,128)(4,1)S(1)} %fusion.24), kind=kLoop, calls=%fused_computation.8 | loop fusion | flops 11780352 | bytes 8317952 | tf_op jit(solution)/shard_map/reduce_sum | solution.py:101
  186.0 2.4 fusion.71
  188.4 1.5 gather_fusion
  190.0 1.2 compare_reduce_fusion
  191.3 70.5 %reduce-scatter.2.cloned.1.call-done = f32[1,128,256]{2,1,0:T(8,128)} async-done(((f32[8,128,256]{2,1,0:T(8,128)}), f32[1,128,256]{2,1,0:T(8,128)}) %reduce-scatter.2.cloned.1.call-update) | async-done | bytes 131088 | tf_op jit(solution)/shard_map/reduce_scatter | solution.py:69
  261.8 0.8 bitcast_convert_fusion
  262.6 0.7 copy.58
  263.3 1.2 fusion.58
  265.0 0.7 pad_maximum_fusion
  265.8 2.9 fusion.72
  269.0 1.0 multiply_reduce_fusion
  270.0 7.5 %fusion = f32[128,6,128]{2,0,1:T(8,128)} fusion(f32[128,6,20]{0,1,2:T(8,128)S(1)} %get-tuple-element.23, f32[20,128,128,6]{2,1,3,0:T(8,128)} %copy-done.1, f32[128,6,20]{0,1,2:T(8,128)} %copy-done.4, pred[128,20,128]{0,2,1:T(8,128)(4,1)} %copy-done.3, bf16[20,1,128,128]{3,2,1,0:T(8,128)(2,1)} %param.16), kind=kOutput, calls=%fused_computation.5 | convolution fusion | flops 516980736 | bytes 9363456 | tf_op jit(solution)/shard_map/rgqpt,pgtd->rgqpd/dot_general | solution.py:102
  277.5 1.9 copy.59
  280.3 0.9 convolution_add_fusion.1
  281.2 2.3 fusion.30
  283.5 1.5 fusion.26
  285.0 0.8 copy.62
  (43 shorter events, 2.2 us)
Async XLA Ops:
  7.2 166.9 %copy-start = (bf16[768,8,256]{2,1,0:T(8,128)(2,1)S(1)}, bf16[768,8,256]{2,1,0:T(8,128)(2,1)}, u32[]{:S(2)}) copy-start(bf16[768,8,256]{2,1,0:T(8,128)(2,1)} %param.13) | copy-start | bytes 9437188
  9.6 31.4 %all-to-all-start = ((s32[64,1,1]{2,1,0:T(1,128)}), s32[64,1,1]{2,1,0:T(1,128)S(1)}, u32[]{:S(2)}, u32[]{:S(2)}) async-start(s32[64,1,1]{2,1,0:T(1,128)} %copy.54), calls=%async_computation.1 | async-start | bytes 65536 | tf_op jit(solution)/shard_map/all_to_all | solution.py:123
  27.8 123.9 %copy-start.7 = (bf16[768]{0:T(1024)(128)(2,1)S(1)}, bf16[768]{0:T(1024)(128)(2,1)}, u32[]{:S(2)}) copy-start(bf16[768]{0:T(1024)(128)(2,1)} %param.12) | copy-start | bytes 4612
  41.0 100.8 %all-to-all-start.1 = ((bf16[64,1,128,128]{3,2,1,0:T(8,128)(2,1)}), bf16[64,1,128,128]{3,2,1,0:T(8,128)(2,1)}, u32[]{:S(2)}, u32[]{:S(2)}) async-start(bf16[64,1,128,128]{3,2,1,0:T(8,128)(2,1)} %bitcast.95), calls=%async_computation.2 | async-start | bytes 4194304 | tf_op jit(solution)/shard_map/all_to_all | solution.py:121
  46.5 130.2 %copy-start.8 = (s32[128]{0:T(128)S(1)}, s32[128]{0:T(128)}, u32[]{:S(2)}) copy-start(s32[128]{0:T(128)} %param.18) | copy-start | bytes 1540
  46.5 130.2 %copy-start.5 = (s32[128,12]{0,1:T(8,128)S(1)}, s32[128,12]{0,1:T(8,128)}, u32[]{:S(2)}) copy-start(s32[128,12]{0,1:T(8,128)} %param.17) | copy-start | bytes 18436
  46.5 130.5 %copy-start.2 = (bf16[128,6,128]{2,0,1:T(8,128)(2,1)S(1)}, bf16[128,6,128]{2,0,1:T(8,128)(2,1)}, u32[]{:S(2)}) copy-start(bf16[128,6,128]{2,0,1:T(8,128)(2,1)} %param.14) | copy-start | bytes 589828
  141.8 139.4 %all-to-all-start.2 = ((bf16[64,1,128,128]{3,2,1,0:T(8,128)(2,1)}), bf16[64,1,128,128]{3,2,1,0:T(8,128)(2,1)}, u32[]{:S(2)}, u32[]{:S(2)}) async-start(bf16[64,1,128,128]{3,2,1,0:T(8,128)(2,1)} %bitcast.94), calls=%async_computation.3 | async-start | bytes 4194304 | tf_op jit(solution)/shard_map/all_to_all | solution.py:122
  151.7 110.1 %reduce-scatter.2.cloned.1.call-start = ((), (), s32[]{:S(2)}) async-start(), calls=%async_computation.4 | async-start | bytes 1179648 | tf_op jit(solution)/shard_map/reduce_scatter | solution.py:69
  177.1 9.0 %copy-start.3 = (pred[128,20,128]{0,2,1:T(8,128)(4,1)}, pred[128,20,128]{0,2,1:T(8,128)(4,1)S(1)}, u32[]{:S(2)}) copy-start(pred[128,20,128]{0,2,1:T(8,128)(4,1)S(1)} %fusion.24) | copy-start | bytes 983044
  179.7 3.1 %copy-start.1 = (f32[20,128,128,6]{2,1,3,0:T(8,128)}, f32[20,128,128,6]{2,1,3,0:T(8,128)S(1)}, u32[]{:S(2)}) copy-start(f32[20,128,128,6]{2,1,3,0:T(8,128)S(1)} %get-tuple-element.27) | copy-start | bytes 23592964
  179.7 8.7 %copy-start.4 = (f32[128,6,20]{0,1,2:T(8,128)}, f32[128,6,20]{0,1,2:T(8,128)S(1)}, u32[]{:S(2)}) copy-start(f32[128,6,20]{0,1,2:T(8,128)S(1)} %get-tuple-element.26) | copy-start | bytes 184324
  188.4 80.6 %copy-start.6 = (s32[64]{0:T(128)}, s32[64]{0:T(128)S(1)}, u32[]{:S(2)}) copy-start(s32[64]{0:T(128)S(1)} %get-tuple-element.14) | copy-start | bytes 772
Sparse Core Ops, SparseCore 0:
  176.8 84.9 reduce-scatter.1
where the time goes:
time: 294 us; the launch traced here: 293 us
  waiting for transfers between devices  172 us (59%)
  starting transfers between devices  33.5 us (11%)
  blocking collectives  21.3 us (7%)
  matrix products  20.6 us (7%)
  local copies, waits for them, and re-layouts  16.2 us (6%)
  other arithmetic  14.4 us (5%)
  between operations  14.3 us (5%)
    all_to_all x1, waiting for transfers between devices, body(): lax.all_to_all(pool_keys[source_page], 'inst', split_axis=0, concat_axis=...  92 us
    reduce_scatter x1, waiting for transfers between devices, body(): lax.psum_scatter(jnp.einsum('rf,fgc->grc', normed, kv_weight, preferred_e...  70.5 us
    psum x1, blocking collectives, body(): squares = lax.psum(jnp.sum(widened * widened, axis=1), 'tp')  21.3 us
    all_to_all x1, starting transfers between devices, body(): lax.all_to_all(label_out, 'inst', split_axis=0, concat_axis=0, tiled=True)  18.2 us
    all_to_all x1, waiting for transfers between devices, body(): lax.all_to_all(label_out, 'inst', split_axis=0, concat_axis=0, tiled=True)  9.94 us
    all_to_all x1, starting transfers between devices, body(): lax.all_to_all(pool_values[source_page], 'inst', split_axis=0, concat_axi...  9.82 us
    dot_general x1, matrix products, body(): jnp.einsum('rgqpt,pgtd->rgqpd', local_weights.astype(jnp.bfloat16), pool_...  7.52 us
  transfers between devices with their start and end apart: 4, of which 3 were waited for; matrix products, arithmetic and copies ran while one was open for 14% of the time, Pallas kernels for 0%

commit v1 on v0

v1 whole, which is shorter than its diff:
```python
import functools
import math

import jax
import jax.numpy as jnp
from jax import lax
from jax.experimental import pallas as pl
from jax.experimental.pallas import tpu as pltpu
from jax.sharding import PartitionSpec as P

EPSILON = 1e-05
ROPE_BASE = 1000000.0
FLOOR = -1e30
WAIT = 6 * 10**9
LANES = 128
SLOTS = 8
LOG2E = 1.4426950408889634
VMEM = pl.BlockSpec(memory_space=pltpu.VMEM)
SMEM = pl.BlockSpec(memory_space=pltpu.SMEM)
ANY = pl.BlockSpec(memory_space=pl.ANY)
HBM = pl.BlockSpec(memory_space=pltpu.HBM)
F32 = jnp.float32
BF16 = jnp.bfloat16
NT = (((1,), (1,)), ((), ()))


def split_three(x):
    first = x.astype(BF16).astype(F32)
    second = (x - first).astype(BF16).astype(F32)
    third = (x - first - second).astype(BF16).astype(F32)
    return first, second, third


def slot_of(code, bits, root, slots):
    return lax.rem((code >> sum(bits)) + (slots - root), slots)


def label_kernel(bits, root, plan_ref, label_ref):
    label_ref[...] = jnp.full(label_ref.shape, -1, jnp.int32)
    for m in range(plan_ref.shape[0]):
        code = plan_ref[m]
        slot = slot_of(code, bits, root, label_ref.shape[0])
        request = (code >> bits[1]) & ((1 << bits[0]) - 1)
        label_ref[slot] = jnp.full((1, LANES), request, jnp.int32)


def ask_kernel(label_ref, query_ref, *rest):
    asked_ref = rest[-1]
    heads, requests, width = query_ref.shape
    slots = asked_ref.shape[0]
    labels = label_ref[...].reshape(slots, LANES)
    chosen = labels == lax.broadcasted_iota(jnp.int32, (slots, requests), 1)
    chosen = jnp.where(chosen, 1.0, 0.0).astype(BF16)
    rows = [jnp.dot(chosen, query_ref[h], preferred_element_type=F32) for h in range(heads)]
    rows += [jnp.zeros((slots, width), F32)] * (SLOTS - heads)
    asked_ref[...] = jnp.swapaxes(jnp.stack(rows), 0, 1).astype(BF16)


def moved_kernel(scale, heads, bits, root, plan_ref, asked_ref, key_ref, value_ref, *rest):
    out_ref, score_ref = rest[-2:]
    moves = plan_ref.shape[0]
    slots = [slot_of(plan_ref[m], bits, root, out_ref.shape[0]) for m in range(moves)]
    pages = [plan_ref[m] & ((1 << bits[1]) - 1) for m in range(moves)]
    for m in range(moves):
        score_ref[m] = lax.dot_general(
            asked_ref[slots[m]], key_ref[pages[m]], NT, preferred_element_type=F32
        )
    scores = score_ref[...] * scale
    highest = jnp.max(scores, axis=-1, keepdims=True)
    weights = jnp.exp2(scores - highest)
    sums = jnp.sum(weights, axis=-1, keepdims=True)
    level = jnp.broadcast_to(highest + jnp.log(sums) * LOG2E, scores.shape)
    row = lax.broadcasted_iota(jnp.int32, scores.shape, 1)
    lane = lax.broadcasted_iota(jnp.int32, scores.shape, 2)
    level = jnp.sum(
        jnp.where((lane % SLOTS == row) & (row < heads), level, 0.0), axis=1, keepdims=True
    )
    first, second, third = split_three(jnp.broadcast_to(level, scores.shape))
    part = lane // SLOTS
    stats = jnp.where(part == 0, first, jnp.where(part == 1, second, third))
    inverse = 1.0 / sums
    rounded = weights.astype(BF16)
    out_ref[...] = jnp.zeros(out_ref.shape, out_ref.dtype)
    for m in range(moves):
        product = jnp.dot(rounded[m], value_ref[pages[m]], preferred_element_type=F32)
        product = product * inverse[m]
        message = jnp.where(row[m] < heads, product, stats[m])
        out_ref[slots[m]] = message.astype(BF16)


def local_kernel(scale, first, query_ref, key_ref, value_ref, table_ref, length_ref, out_ref, stat_ref, bias_ref, score_ref):
    heads, requests, width = out_ref.shape
    pool, page_len, _ = key_ref.shape
    pairs = pool // 2
    entries = table_ref.shape[0]
    lengths = length_ref[...]
    page = lax.broadcasted_iota(jnp.int32, (LANES, requests), 0)
    counts = jnp.zeros((LANES, requests), jnp.int32)
    for i in range(entries):
        held = jnp.clip(lengths - i * page_len, 0, page_len)
        counts = counts + jnp.where(table_ref[i : i + 1, :] == page, held, 0)
    counts = counts.astype(F32).T
    token = lax.broadcasted_iota(jnp.int32, (requests, page_len), 1).astype(F32)
    for p in range(pool):
        bias_ref[p // 2, :, (p % 2) * page_len : (p % 2 + 1) * page_len] = jnp.where(
            token < counts[:, p : p + 1], 0.0, FLOOR
        )
    query = query_ref[first : first + heads].reshape(heads * requests, width)
    best = jnp.full((heads, requests, 2 * page_len), FLOOR, F32)
    for p in range(pairs):
        keys = key_ref[2 * p : 2 * p + 2].reshape(2 * page_len, width)
        scores = lax.dot_general(query, keys, NT, preferred_element_type=F32)
        scores = scores.reshape(heads, requests, 2 * page_len) * scale + bias_ref[p][None]
        score_ref[p] = scores
        best = jnp.maximum(best, scores)
    best = jnp.max(best, axis=-1, keepdims=True)
    total = jnp.zeros((heads, requests, 2 * page_len), F32)
    out = jnp.zeros((heads * requests, width), F32)
    for p in range(pairs):
        values = value_ref[2 * p : 2 * p + 2].reshape(2 * page_len, width)
        weights = jnp.exp2(score_ref[p] - best)
        total = total + weights
        rounded = weights.astype(BF16).reshape(heads * requests, 2 * page_len)
        out = out + jnp.dot(rounded, values, preferred_element_type=F32)
    out_ref[...] = out.reshape(heads, requests, width)
    total = jnp.sum(total, axis=-1, keepdims=True)
    lane = lax.broadcasted_iota(jnp.int32, (requests, LANES), 1)
    stats = jnp.zeros((requests, LANES), F32)
    for h in range(heads):
        stats = jnp.where(lane == first + h, best[h], stats)
        stats = jnp.where(lane == SLOTS + first + h, total[h], stats)
    stat_ref[...] = stats


def norm_kernel(hidden_ref, gain_ref, _, scaled_ref, extra_ref):
    widened = hidden_ref[...].astype(F32)
    requests = widened.shape[0]
    scaled_ref[...] = (widened * gain_ref[...].astype(F32).reshape(1, -1)).astype(BF16)
    squares = jnp.sum(widened * widened, axis=1, keepdims=True)
    row = lax.broadcasted_iota(jnp.int32, (requests, LANES), 0)
    lane = lax.broadcasted_iota(jnp.int32, (requests, LANES), 1)
    squares = jnp.sum(jnp.where(row == lane, squares, 0.0), axis=0, keepdims=True)
    first, second, third = split_three(squares)
    upper = jnp.concatenate([first, second], axis=1)
    lower = jnp.concatenate([third, jnp.zeros_like(third)], axis=1)
    place = lax.broadcasted_iota(jnp.int32, extra_ref.shape, 0) - 2 * lax.axis_index("tp")
    extra_ref[...] = jnp.where(place == 0, upper, jnp.where(place == 1, lower, 0.0))


def bits():
    rank = lax.axis_index("tp")
    return rank // 2 % 2, rank // 4, rank % 2


def first_kernel(partial_ref, extra_ref, send_ref, keep_ref):
    near, _, _ = bits()
    rows = partial_ref.shape[1]
    for i in range(2):
        for j in range(2):
            keep_ref[i, j, :rows] = partial_ref[4 * i + 2 * near + j]
            keep_ref[i, j, rows:] = extra_ref[...]
            send_ref[i, j, :rows] = partial_ref[4 * i + 2 * (1 - near) + j].astype(BF16)
            send_ref[i, j, rows:] = extra_ref[...].astype(BF16)


def second_kernel(got_ref, kept_ref, _, send_ref, keep_ref):
    _, far, _ = bits()
    keep_ref[...] = kept_ref[far] + got_ref[far].astype(F32)
    send_ref[...] = (kept_ref[1 - far] + got_ref[1 - far].astype(F32)).astype(BF16)


def third_kernel(got_ref, keep_ref, _, send_ref, last_ref):
    mid = bits()[2]
    last_ref[...] = keep_ref[mid] + got_ref[mid].astype(F32)
    send_ref[...] = (keep_ref[1 - mid] + got_ref[1 - mid].astype(F32)).astype(BF16)


def fresh_kernel(scale, features, got_ref, last_ref, cos_ref, sin_ref, query_ref, out_a_ref, stat_a_ref, out_b_ref, stat_b_ref, kv_ref, new_out_ref, new_stat_ref):
    heads, requests, width = query_ref.shape
    part = out_a_ref.shape[0]
    total = last_ref[...] + got_ref[...].astype(F32)
    extra = jnp.sum(total[requests:], axis=0, keepdims=True)
    squares = extra[:, :LANES] + extra[:, LANES:]
    row = lax.broadcasted_iota(jnp.int32, (requests, LANES), 0)
    lane = lax.broadcasted_iota(jnp.int32, (requests, LANES), 1)
    squares = jnp.sum(jnp.where(row == lane, squares, 0.0), axis=1, keepdims=True)
    inverse = lax.rsqrt(squares / features + EPSILON)
    projected = total[:requests] * inverse
    key = projected[:, :width]
    key = key * cos_ref[...] + pltpu.roll(key, width // 2, 1) * sin_ref[...]
    key = key.astype(BF16)
    value = projected[:, width:].astype(BF16)
    kv_ref[:, :width] = key
    kv_ref[:, width:] = value
    key = key.astype(F32)
    value = value.astype(F32)
    stats = stat_a_ref[...] + stat_b_ref[...]
    new_stats = jnp.zeros((requests, LANES), F32)
    for h in range(heads):
        score = jnp.sum(query_ref[h].astype(F32) * key, axis=1, keepdims=True) * scale
        highest = stats[:, h : h + 1]
        best = jnp.maximum(highest, score)
        factor = jnp.exp2(highest - best)
        fresh = jnp.exp2(score - best)
        out = out_a_ref[h] if h < part else out_b_ref[h - part]
        new_out_ref[h] = out * factor + fresh * value
        sums = stats[:, SLOTS + h : SLOTS + h + 1] * factor + fresh
        new_stats = jnp.where(lane == h, best, new_stats)
        new_stats = jnp.where(lane == SLOTS + h, sums, new_stats)
    new_stat_ref[...] = new_stats


def owner_kernel(label_ref, owner_ref):
    requests, slots = owner_ref.shape
    labels = label_ref[...].reshape(slots, LANES).T
    owner_ref[...] = jnp.where(
        labels == lax.broadcasted_iota(jnp.int32, (requests, slots), 0), 0.0, FLOOR
    )


def combine_kernel(message_ref, owner_ref, out_ref, stat_ref, final_ref):
    heads, requests, width = out_ref.shape
    messages = jnp.swapaxes(message_ref[...].astype(F32), 0, 1)
    levels = messages[heads].T
    levels = levels[0:SLOTS] + levels[SLOTS : 2 * SLOTS] + levels[2 * SLOTS : 3 * SLOTS]
    bias = owner_ref[...]
    stats = stat_ref[...]
    for h in range(heads):
        scores = bias + levels[h : h + 1]
        highest = stats[:, h : h + 1]
        best = jnp.maximum(highest, jnp.max(scores, axis=1, keepdims=True))
        weights = jnp.exp2(scores - best)
        factor = jnp.exp2(highest - best)
        sums = stats[:, SLOTS + h : SLOTS + h + 1] * factor + jnp.sum(weights, axis=1, keepdims=True)
        coarse = weights.astype(BF16)
        fine = (weights - coarse.astype(F32)).astype(BF16)
        moved = messages[h].astype(BF16)
        total = (
            out_ref[h] * factor
            + jnp.dot(coarse, moved, preferred_element_type=F32)
            + jnp.dot(fine, moved, preferred_element_type=F32)
        )
        final_ref[:, h * width : (h + 1) * width] = (total / sums).astype(BF16)


def call(kernel, shapes, ins, scratch=(), limit=8, flops=10**9, moved=0):
    return pl.pallas_call(
        kernel,
        out_shape=shapes,
        in_specs=ins,
        out_specs=jax.tree.map(lambda _: VMEM, shapes),
        scratch_shapes=scratch,
        compiler_params=pltpu.CompilerParams(vmem_limit_bytes=limit * 1024 * 1024),
        cost_estimate=pl.CostEstimate(flops=flops, bytes_accessed=moved, transcendentals=0),
    )


def rotation(lengths, width):
    steps = jnp.arange(width // 2, dtype=F32)
    frequency = ROPE_BASE ** (-2.0 * steps / width)
    angles = lengths.astype(F32)[:, None] * frequency[None, :]
    cosine = jnp.cos(angles)
    sine = jnp.sin(angles)
    return jnp.concatenate([cosine, cosine], axis=1), jnp.concatenate([-sine, sine], axis=1)


def body(
    hidden_state,
    norm_gain,
    kv_weight,
    queries,
    pool_keys,
    pool_values,
    page_table,
    lengths,
    move_target,
    move_page,
    move_request,
):
    shape = jax.ShapeDtypeStruct
    requests, heads, width = queries.shape
    pool, _, page_len, _ = pool_keys.shape
    moves = move_page.shape[0]
    instances = lax.axis_size("inst")
    ranks = lax.axis_size("tp")
    features = hidden_state.shape[1] * ranks
    scale = LOG2E / math.sqrt(width)
    root = instances * 25 // 32
    order = [(i + root) % instances for i in range(instances)]

    def exchange(x):
        return lax.all_to_all(x, "inst", 0, 0, tiled=True, axis_index_groups=[order])


    def swap(x, bit):
        return lax.ppermute(x, "tp", [(i, i ^ bit) for i in range(ranks)])

    keys = pool_keys.reshape(pool, page_len, width)
    values = pool_values.reshape(pool, page_len, width)
    by_head = jnp.transpose(queries, (1, 0, 2))

    bits = ((requests - 1).bit_length(), (pool - 1).bit_length())
    plan = (((move_target[:, 0] << bits[0]) | move_request) << bits[1]) | move_page
    labels = call(
        functools.partial(label_kernel, bits, root),
        shape((instances, 1, LANES), jnp.int32),
        [SMEM],
        flops=10**10,
    )(plan)
    labels = exchange(labels)

    scaled, extra = call(
        norm_kernel,
        [shape(hidden_state.shape, BF16), shape((16, 2 * width), F32)],
        [VMEM, VMEM, ANY],
    )(hidden_state, norm_gain, kv_weight)
    partial = jnp.einsum("rf,fgc->grc", scaled, kv_weight, preferred_element_type=F32)
    padded = requests + 16
    send, keep = call(
        first_kernel,
        [shape((2, 2, padded, 2 * width), BF16), shape((2, 2, padded, 2 * width), F32)],
        [VMEM, VMEM],
    )(partial, extra)
    got = swap(send, 2)

    def local(first, count, weight):
        return call(
            functools.partial(local_kernel, scale, first),
            [shape((count, requests, width), F32), shape((requests, LANES), F32)],
            [VMEM] * 5,
            [
                pltpu.VMEM((pool // 2, requests, 2 * page_len), F32),
                pltpu.VMEM((pool // 2, count, requests, 2 * page_len), F32),
            ],
            limit=16,
            flops=4 * weight * count * requests * pool * page_len * width,
            moved=4 * pool * page_len * width,
        )(by_head, keys, values, page_table.T, lengths[None, :])

    asked = call(ask_kernel, shape((instances, SLOTS, width), BF16), [VMEM, VMEM, ANY])(labels, by_head, send)
    asked = exchange(asked)

    out_a, stat_a = local(0, heads // 2, 12)
    send, keep = call(
        second_kernel,
        [shape((2, padded, 2 * width), BF16), shape((2, padded, 2 * width), F32)],
        [VMEM, VMEM, ANY],
    )(got, keep, stat_a)
    got = swap(send, 4)

    answers = call(
        functools.partial(moved_kernel, scale, heads, bits, root),
        shape((instances, SLOTS, width), BF16),
        [SMEM, VMEM, VMEM, VMEM, ANY],
        [pltpu.VMEM((moves, SLOTS, page_len), F32)],
    )(plan, asked, keys, values, send)
    answers = exchange(answers)

    owner = call(
        owner_kernel, shape((requests, instances), F32), [VMEM], flops=WAIT
    )(labels)
    out_b, stat_b = local(heads // 2, heads - heads // 2, 1)
    send, last = call(
        third_kernel,
        [shape((padded, 2 * width), BF16), shape((padded, 2 * width), F32)],
        [VMEM, VMEM, ANY],
    )(got, keep, owner)
    got = swap(send, 1)
    cosine, sine = rotation(lengths, width)
    new_kv, out, stats = call(
        functools.partial(fresh_kernel, scale, features),
        [
            shape((requests, 2 * width), BF16),
            shape((heads, requests, width), F32),
            shape((requests, LANES), F32),
        ],
        [VMEM] * 9,
    )(got, last, cosine, sine, by_head, out_a, stat_a, out_b, stat_b)
    attention_out = call(combine_kernel, shape((requests, heads * width), BF16), [VMEM] * 4)(
        answers, owner, out, stats
    )
    return (attention_out, new_kv.reshape(requests, 1, 2 * width))


def solution(mesh):
    return jax.shard_map(
        body,
        mesh=mesh,
        in_specs=(
            P("inst", "tp"),
            P("tp"),
            P("tp", None, None),
            P("inst", "tp", None),
            P("inst", "tp", None, None),
            P("inst", "tp", None, None),
            P("inst", None),
            P("inst"),
            P("inst", None),
            P("inst"),
            P("inst"),
        ),
        out_specs=(P("inst", "tp"), P("inst", "tp", None)),
        check_vma=False,
    )
```

time: 294 us -> 79.4 us (0.27)
  waiting for transfers between devices: 172 us -> 0.02 us
  starting transfers between devices: 33.5 us -> 60.7 us
  blocking collectives: 21.3 us -> 0 us
  matrix products: 20.6 us -> 0.66 us
  local copies, waits for them, and re-layouts: 16.2 us -> 0.05 us
  Pallas kernels: 0 us -> 15 us
  between operations: 14.3 us -> 0.91 us
  other arithmetic: 14.4 us -> 1.76 us
    all_to_all x3, waiting for transfers between devices: 102 us -> 0.01 us  [exchange(): lax.all_to_all(x, 'inst', 0, 0, tiled=True, axis_index_groups=[order])]
    reduce_scatter x1 -> x0, waiting for transfers between devices: 70.5 us -> none  [body(): lax.psum_scatter(jnp.einsum('rf,fgc->grc', normed, kv_weight, preferred_e...]
    psum x1 -> x0, blocking collectives: 21.3 us -> none  [body(): squares = lax.psum(jnp.sum(widened * widened, axis=1), 'tp')]
    dot_general x8 -> x1, matrix products: 20.6 us -> 0.66 us  [body(): jnp.einsum('rf,fgc->grc', scaled, kv_weight, preferred_element_type=F32)]
    pallas_call x0 -> x12, Pallas kernels: none -> 15 us  [the longest x2 5.6 us: local(): call(functools.partial(local_kernel, scale, first), [shape((count, reques...]
    all_to_all x3, starting transfers between devices: 33.5 us -> 48.2 us  [exchange(): lax.all_to_all(x, 'inst', 0, 0, tiled=True, axis_index_groups=[order])]
    ppermute x0 -> x3, starting transfers between devices: none -> 12.5 us  [swap(): return lax.ppermute(x, 'tp', [(i, i ^ bit) for i in range(ranks)])]
    gather x4 -> x0, local copies, waits for them, and re-layouts: 8.69 us -> none  [the longest x1 3.34 us: body(): pool_values[source_page]]
  transfers between devices with their start and end apart: 4 -> 6, of which waited for: 3 -> 0; matrix products, arithmetic and copies ran while one was open for 14% -> 2% of each run, Pallas kernels for 0% -> 14%
where the time goes in v1:
time: 79.4 us; the launch traced here: 79.1 us
  starting transfers between devices  60.7 us (76%)
  Pallas kernels  15 us (19%)
  other arithmetic  1.76 us (2%)
  between operations  0.91 us (1%)
    all_to_all x3, starting transfers between devices, exchange(): lax.all_to_all(x, 'inst', 0, 0, tiled=True, axis_index_groups=[order])  48.2 us
    ppermute x3, starting transfers between devices, swap(): return lax.ppermute(x, 'tp', [(i, i ^ bit) for i in range(ranks)])  12.5 us
    pallas_call x2, Pallas kernels, local(): call(functools.partial(local_kernel, scale, first), [shape((count, reques...  5.6 us
    pallas_call x1, Pallas kernels, body(): call(combine_kernel, shape((requests, heads * width), BF16), [VMEM] * 4)  2.49 us
    pallas_call x1, Pallas kernels, body(): call(functools.partial(fresh_kernel, scale, features), [shape((requests,...  2.16 us
    pallas_call x1, Pallas kernels, body(): call(functools.partial(moved_kernel, scale, heads, bits, root), shape((in...  2.14 us
  transfers between devices with their start and end apart: 6, of which 0 were waited for; matrix products, arithmetic and copies ran while one was open for 2% of the time, Pallas kernels for 14%

profile of v1, /device:TPU:1, one launch (start us, length us, event | category | flops | bytes accessed | tf_op | source)
XLA Modules:
  0.0 79.1 jit_solution(12559574540730213628)
XLA Ops:
  0.6 0.7 fusion.8.plan_ref
  1.3 1.3 %shard_map.122 = s32[64,1,128]{2,1,0:T(1,128)} custom-call(s32[32]{0:T(128)S(1)} %fusion.8.plan_ref), custom_call_target="tpu_custom_call" | custom-call | flops 10000000000 | tf_op jit(solution)/shard_map/pallas_call | solution.py:304
  2.6 20.7 %all-to-all-start = ((s32[64,1,128]{2,1,0:T(1,128)}), s32[64,1,128]{2,1,0:T(1,128)S(1)}, u32[]{:S(2)}, u32[]{:S(2)}) async-start(s32[64,1,128]{2,1,0:T(1,128)} %shard_map.122), calls=%async_computation | async-start | bytes 65536 | tf_op jit(solution)/shard_map/all_to_all | solution.py:292
  23.3 0.2 shard_map.123
  23.5 0.7 fusion.2.partial_ref
  24.1 0.0 copy-start.1
  24.1 0.0 copy-start.2
  24.1 0.0 copy-start.5
  24.2 0.0 copy-start.7
  24.2 0.1 shard_map.124
  24.3 3.2 %collective-permute-start = (bf16[2,2,144,256]{3,2,1,0:T(8,128)(2,1)S(1)}, bf16[2,2,144,256]{3,2,1,0:T(8,128)(2,1)S(1)}, u32[]{:S(2)}, u32[]{:S(2)}) collective-permute-start(bf16[2,2,144,256]{3,2,1,0:T(8,128)(2,1)S(1)} %get-tuple-element.19.rest_0_), channel_id=1, source_target_pairs={{0,2},{1,3},{2,0},{3,1},{4,6},{5,7},{6,4},{7,5},{8,10},{9,11},{10,... | collective-permute-start | bytes 884744 | tf_op jit(solution)/shard_map/ppermute | solution.py:296
  27.5 0.0 all-to-all-done.label_ref
  27.5 0.9 %shard_map.125 = bf16[64,8,128]{2,1,0:T(8,128)(2,1)} custom-call(s32[64,1,128]{2,1,0:T(1,128)S(1)} %all-to-all-done.label_ref, bf16[6,128,128]{2,1,0:T(8,128)(2,1)S(1)} %bitcast.23, bf16[2,2,144,256]{3,2,1,0:T(8,128)(2,1)S(1)} %get-tuple-element.19.rest_0_), custom_call_target="tpu_custom_call" | custom-call | flops 1000000000 | tf_op jit(solution)/shard_map/pallas_call | solution.py:340
  28.4 13.8 %all-to-all-start.1 = ((bf16[64,8,128]{2,1,0:T(8,128)(2,1)}), bf16[64,8,128]{2,1,0:T(8,128)(2,1)S(1)}, u32[]{:S(2)}, u32[]{:S(2)}) async-start(bf16[64,8,128]{2,1,0:T(8,128)(2,1)} %shard_map.125), calls=%async_computation.1 | async-start | bytes 262144 | tf_op jit(solution)/shard_map/all_to_all | solution.py:292
  42.2 2.8 %shard_map.126 = (f32[3,128,128]{2,1,0:T(8,128)S(1)}, f32[128,128]{1,0:T(8,128)S(1)}) custom-call(bf16[6,128,128]{2,1,0:T(8,128)(2,1)S(1)} %bitcast.24, bf16[20,128,128]{2,1,0:T(8,128)(2,1)S(1)} %bitcast.17, bf16[20,128,128]{2,1,0:T(8,128)(2,1)S(1)} %bitcast.20, s32[12,128]{1,0:T(8,128)S(1)} %bitcast.27, s32[1,128]{1,0:T(1,128)S(1)} %bitcast.29), custom_call_target="tpu_custom_call" | custom-call | flops 6039797760 | bytes 1310720 | tf_op jit(solution)/shard_map/pallas_call | solution.py:327
  45.0 1.0 %fusion.6 = (f32[128,64]{1,0:T(8,128)S(1)}, f32[128,64]{1,0:T(8,128)}, f32[128,64]{1,0:T(8,128)}) fusion(f32[64]{0:T(128)S(1)} %multiply_power_fusion, f32[128]{0:T(128)S(1)} %convert_element_type.3), kind=kLoop, calls=%fused_computation.8 | loop fusion | flops 16384 | bytes 99072 | tf_op jit(solution)/shard_map/neg | solution.py:264
  46.0 0.0 collective-permute-done.got_ref
  46.0 0.1 shard_map.127
  46.1 4.4 %collective-permute-start.1 = (bf16[2,144,256]{2,1,0:T(8,128)(2,1)S(1)}, bf16[2,144,256]{2,1,0:T(8,128)(2,1)S(1)}, u32[]{:S(2)}, u32[]{:S(2)}) collective-permute-start(bf16[2,144,256]{2,1,0:T(8,128)(2,1)S(1)} %get-tuple-element.22.rest_0_), channel_id=1, source_target_pairs={{0,4},{1,5},{2,6},{3,7},{4,0},{5,1},{6,2},{7,3},{8,12},{9,13},{10,... | collective-permute-start | bytes 442376 | tf_op jit(solution)/shard_map/ppermute | solution.py:296
  50.4 0.0 all-to-all-done.1.asked_ref
  50.4 2.1 %shard_map.128 = bf16[64,8,128]{2,1,0:T(8,128)(2,1)} custom-call(s32[32]{0:T(128)S(1)} %fusion.8.plan_ref, bf16[64,8,128]{2,1,0:T(8,128)(2,1)S(1)} %all-to-all-done.1.asked_ref, bf16[20,128,128]{2,1,0:T(8,128)(2,1)S(1)} %bitcast.18, bf16[20,128,128]{2,1,0:T(8,128)(2,1)S(1)} %bitcast.21, bf16[2,144,256]{2,1,0:T(8,128)(2,1)S(1)} %get-tuple-element.22.rest_0_), custom_call_target="tpu_custom_call" | custom-call | flops 1000000000 | tf_op jit(solution)/shard_map/pallas_call | solution.py:351
  52.6 13.8 %all-to-all-start.2 = ((bf16[64,8,128]{2,1,0:T(8,128)(2,1)}), bf16[64,8,128]{2,1,0:T(8,128)(2,1)S(1)}, u32[]{:S(2)}, u32[]{:S(2)}) async-start(bf16[64,8,128]{2,1,0:T(8,128)(2,1)} %shard_map.128), calls=%async_computation.2 | async-start | bytes 262144 | tf_op jit(solution)/shard_map/all_to_all | solution.py:292
  66.4 0.1 shard_map.129._.owner_ref
  66.5 0.0 copy-start.8
  66.5 0.0 collective-permute-done.1.got_ref
  66.5 0.1 shard_map.130
  66.6 4.9 %collective-permute-start.2 = (bf16[144,256]{1,0:T(8,128)(2,1)S(1)}, bf16[144,256]{1,0:T(8,128)(2,1)S(1)}, u32[]{:S(2)}, u32[]{:S(2)}) collective-permute-start(bf16[144,256]{1,0:T(8,128)(2,1)S(1)} %get-tuple-element.24), channel_id=1, source_target_pairs={{0,1},{1,0},{2,3},{3,2},{4,5},{5,4},{6,7},{7,6},{8,9},{9,8},{10,11... | collective-permute-start | bytes 221192 | tf_op jit(solution)/shard_map/ppermute | solution.py:296
  71.5 0.1 pad_maximum_fusion
  71.6 2.8 %shard_map.131 = (f32[3,128,128]{2,1,0:T(8,128)S(1)}, f32[128,128]{1,0:T(8,128)S(1)}) custom-call(bf16[6,128,128]{2,1,0:T(8,128)(2,1)S(1)} %bitcast.25, bf16[20,128,128]{2,1,0:T(8,128)(2,1)S(1)} %bitcast.19, bf16[20,128,128]{2,1,0:T(8,128)(2,1)S(1)} %bitcast.22, s32[12,128]{1,0:T(8,128)S(1)} %bitcast.28, s32[1,128]{1,0:T(1,128)S(1)} %bitcast.30), custom_call_target="tpu_custom_call" | custom-call | flops 503316480 | bytes 1310720 | tf_op jit(solution)/shard_map/pallas_call | solution.py:327
  74.4 0.0 collective-permute-done.2.got_ref
  74.4 2.2 %shard_map.132 = (bf16[128,256]{1,0:T(8,128)(2,1)}, f32[6,128,128]{2,1,0:T(8,128)S(1)}, f32[128,128]{1,0:T(8,128)S(1)}) custom-call(bf16[144,256]{1,0:T(8,128)(2,1)S(1)} %collective-permute-done.2.got_ref, f32[144,256]{1,0:T(8,128)S(1)} %get-tuple-element.25.last_ref, f32[128,128]{1,0:T(8,128)S(1)} %get-tuple-element.35.cos_ref, ...), custom_call_target="tpu_custom_call" | custom-call | flops 1000000000 | tf_op jit(solution)/shard_map/pallas_call | solution.py:370
  76.6 2.5 %shard_map.133 = bf16[128,768]{1,0:T(8,128)(2,1)} custom-call(bf16[64,8,128]{2,1,0:T(8,128)(2,1)S(1)} %all-to-all-done.2.message_ref, f32[128,64]{1,0:T(8,128)S(1)} %shard_map.129._.owner_ref, f32[6,128,128]{2,1,0:T(8,128)S(1)} %get-tuple-element.29.out_ref, f32[128,128]{1,0:T(8,128)S(1)} %get-tuple-element.30.stat_ref), custom_call_target="tpu_custom_call" | custom-call | flops 1000000000 | tf_op jit(solution)/shard_map/pallas_call | solution.py:379
  (18 shorter events, 0.0 us)
Async XLA Ops:
  1.3 21.9 %copy-start = (bf16[768,8,256]{2,1,0:T(8,128)(2,1)S(1)}, bf16[768,8,256]{2,1,0:T(8,128)(2,1)}, u32[]{:S(2)}) copy-start(bf16[768,8,256]{2,1,0:T(8,128)(2,1)} %_.1) | copy-start | bytes 9437188
  1.3 21.9 %copy-start.3 = (bf16[128,768]{1,0:T(8,128)(2,1)S(1)}, bf16[128,768]{1,0:T(8,128)(2,1)}, u32[]{:S(2)}) copy-start(bf16[128,768]{1,0:T(8,128)(2,1)} %hidden_ref.1) | copy-start | bytes 589828
  1.3 22.0 %copy-start.6 = (bf16[768]{0:T(1024)(128)(2,1)S(1)}, bf16[768]{0:T(1024)(128)(2,1)}, u32[]{:S(2)}) copy-start(bf16[768]{0:T(1024)(128)(2,1)} %gain_ref.1) | copy-start | bytes 4612
  2.6 24.9 %all-to-all-start = ((s32[64,1,128]{2,1,0:T(1,128)}), s32[64,1,128]{2,1,0:T(1,128)S(1)}, u32[]{:S(2)}, u32[]{:S(2)}) async-start(s32[64,1,128]{2,1,0:T(1,128)} %shard_map.122), calls=%async_computation | async-start | bytes 65536 | tf_op jit(solution)/shard_map/all_to_all | solution.py:292
  23.4 4.1 %copy-start.4 = (bf16[128,6,128]{2,0,1:T(8,128)(2,1)S(1)}, bf16[128,6,128]{2,0,1:T(8,128)(2,1)}, u32[]{:S(2)}) copy-start(bf16[128,6,128]{2,0,1:T(8,128)(2,1)} %param.14) | copy-start | bytes 589828
  24.1 18.0 %copy-start.1 = (bf16[20,1,128,128]{3,2,1,0:T(8,128)(2,1)S(1)}, bf16[20,1,128,128]{3,2,1,0:T(8,128)(2,1)}, u32[]{:S(2)}) copy-start(bf16[20,1,128,128]{3,2,1,0:T(8,128)(2,1)} %param.15) | copy-start | bytes 1966084
  24.1 18.0 %copy-start.2 = (bf16[20,1,128,128]{3,2,1,0:T(8,128)(2,1)S(1)}, bf16[20,1,128,128]{3,2,1,0:T(8,128)(2,1)}, u32[]{:S(2)}) copy-start(bf16[20,1,128,128]{3,2,1,0:T(8,128)(2,1)} %param.16) | copy-start | bytes 1966084
  24.1 18.0 %copy-start.5 = (s32[128,12]{0,1:T(8,128)S(1)}, s32[128,12]{0,1:T(8,128)}, u32[]{:S(2)}) copy-start(s32[128,12]{0,1:T(8,128)} %param.17) | copy-start | bytes 18436
  24.2 18.0 %copy-start.7 = (s32[128]{0:T(128)S(1)}, s32[128]{0:T(128)}, u32[]{:S(2)}) copy-start(s32[128]{0:T(128)} %param.18) | copy-start | bytes 1540
  24.3 21.7 %collective-permute-start = (bf16[2,2,144,256]{3,2,1,0:T(8,128)(2,1)S(1)}, bf16[2,2,144,256]{3,2,1,0:T(8,128)(2,1)S(1)}, u32[]{:S(2)}, u32[]{:S(2)}) collective-permute-start(bf16[2,2,144,256]{3,2,1,0:T(8,128)(2,1)S(1)} %get-tuple-element.19.rest_0_), channel_id=1, source_target_pairs={{0,2},{1,3},{2,0},{3,1},{4,6},{5,7},{6,4},{7,5},{8,10},{9,11},{10,... | collective-permute-start | bytes 884744 | tf_op jit(solution)/shard_map/ppermute | solution.py:296
  28.4 22.0 %all-to-all-start.1 = ((bf16[64,8,128]{2,1,0:T(8,128)(2,1)}), bf16[64,8,128]{2,1,0:T(8,128)(2,1)S(1)}, u32[]{:S(2)}, u32[]{:S(2)}) async-start(bf16[64,8,128]{2,1,0:T(8,128)(2,1)} %shard_map.125), calls=%async_computation.1 | async-start | bytes 262144 | tf_op jit(solution)/shard_map/all_to_all | solution.py:292
  46.1 20.4 %collective-permute-start.1 = (bf16[2,144,256]{2,1,0:T(8,128)(2,1)S(1)}, bf16[2,144,256]{2,1,0:T(8,128)(2,1)S(1)}, u32[]{:S(2)}, u32[]{:S(2)}) collective-permute-start(bf16[2,144,256]{2,1,0:T(8,128)(2,1)S(1)} %get-tuple-element.22.rest_0_), channel_id=1, source_target_pairs={{0,4},{1,5},{2,6},{3,7},{4,0},{5,1},{6,2},{7,3},{8,12},{9,13},{10,... | collective-permute-start | bytes 442376 | tf_op jit(solution)/shard_map/ppermute | solution.py:296
  52.6 24.0 %all-to-all-start.2 = ((bf16[64,8,128]{2,1,0:T(8,128)(2,1)}), bf16[64,8,128]{2,1,0:T(8,128)(2,1)S(1)}, u32[]{:S(2)}, u32[]{:S(2)}) async-start(bf16[64,8,128]{2,1,0:T(8,128)(2,1)} %shard_map.128), calls=%async_computation.2 | async-start | bytes 262144 | tf_op jit(solution)/shard_map/all_to_all | solution.py:292
  66.5 5.0 %copy-start.8 = (f32[128,64]{1,0:T(8,128)S(1)}, f32[128,64]{1,0:T(8,128)}, u32[]{:S(2)}) copy-start(f32[128,64]{1,0:T(8,128)} %get-tuple-element.33) | copy-start | bytes 98308
  66.5 5.0 %copy-start.9 = (f32[128,64]{1,0:T(8,128)S(1)}, f32[128,64]{1,0:T(8,128)}, u32[]{:S(2)}) copy-start(f32[128,64]{1,0:T(8,128)} %get-tuple-element.34) | copy-start | bytes 98308
  66.6 7.8 %collective-permute-start.2 = (bf16[144,256]{1,0:T(8,128)(2,1)S(1)}, bf16[144,256]{1,0:T(8,128)(2,1)S(1)}, u32[]{:S(2)}, u32[]{:S(2)}) collective-permute-start(bf16[144,256]{1,0:T(8,128)(2,1)S(1)} %get-tuple-element.24), channel_id=1, source_target_pairs={{0,1},{1,0},{2,3},{3,2},{4,5},{5,4},{6,7},{7,6},{8,9},{9,8},{10,11... | collective-permute-start | bytes 221192 | tf_op jit(solution)/shard_map/ppermute | solution.py:296

commit v2 on v1

--- a/solution.py
+++ b/solution.py
@@ -11,7 +11,9 @@
 EPSILON = 1e-05
 ROPE_BASE = 1000000.0
 FLOOR = -1e30
-WAIT = 6 * 10**9
+SECOND = 0
+THIRD = 10**9
+LATER = 2 * 10**8
 LANES = 128
 SLOTS = 8
 LOG2E = 1.4426950408889634
@@ -22,6 +24,7 @@
 F32 = jnp.float32
 BF16 = jnp.bfloat16
 NT = (((1,), (1,)), ((), ()))
+TN = (((0,), (0,)), ((), ()))
 
 
 def split_three(x):
@@ -36,12 +39,13 @@
 
 
 def label_kernel(bits, root, plan_ref, label_ref):
-    label_ref[...] = jnp.full(label_ref.shape, -1, jnp.int32)
-    for m in range(plan_ref.shape[0]):
-        code = plan_ref[m]
-        slot = slot_of(code, bits, root, label_ref.shape[0])
-        request = (code >> bits[1]) & ((1 << bits[0]) - 1)
-        label_ref[slot] = jnp.full((1, LANES), request, jnp.int32)
+    slots = label_ref.shape[0]
+    plan = plan_ref[...]
+    place = slot_of(plan, bits, root, slots)
+    request = (plan >> bits[1]) & ((1 << bits[0]) - 1)
+    named = place == lax.broadcasted_iota(jnp.int32, (slots, plan.shape[1]), 0)
+    found = jnp.sum(jnp.where(named, request + 1, 0), axis=1, keepdims=True) - 1
+    label_ref[...] = jnp.broadcast_to(found, (slots, LANES)).reshape(slots, 1, LANES)
 
 
 def ask_kernel(label_ref, query_ref, *rest):
@@ -52,18 +56,24 @@
     chosen = labels == lax.broadcasted_iota(jnp.int32, (slots, requests), 1)
     chosen = jnp.where(chosen, 1.0, 0.0).astype(BF16)
     rows = [jnp.dot(chosen, query_ref[h], preferred_element_type=F32) for h in range(heads)]
-    rows += [jnp.zeros((slots, width), F32)] * (SLOTS - heads)
-    asked_ref[...] = jnp.swapaxes(jnp.stack(rows), 0, 1).astype(BF16)
+    halves = [jnp.concatenate(rows[i::2], axis=1) for i in range(2)]
+    asked_ref[...] = jnp.swapaxes(jnp.stack(halves), 0, 1).astype(BF16)
 
 
 def moved_kernel(scale, heads, bits, root, plan_ref, asked_ref, key_ref, value_ref, *rest):
     out_ref, score_ref = rest[-2:]
-    moves = plan_ref.shape[0]
-    slots = [slot_of(plan_ref[m], bits, root, out_ref.shape[0]) for m in range(moves)]
-    pages = [plan_ref[m] & ((1 << bits[1]) - 1) for m in range(moves)]
+    moves = plan_ref.shape[1]
+    width = out_ref.shape[2]
+    plan = [plan_ref[0, m] for m in range(moves)]
+    slots = [slot_of(code, bits, root, out_ref.shape[0]) for code in plan]
+    pages = [code & ((1 << bits[1]) - 1) for code in plan]
+    spare = jnp.zeros((SLOTS - heads, width), F32)
     for m in range(moves):
+        pairs = asked_ref[slots[m]].astype(F32)
+        query = [pairs[:, i * width : (i + 1) * width] for i in range(heads // 2)]
+        query = jnp.concatenate(query + [spare], axis=0).astype(BF16)
         score_ref[m] = lax.dot_general(
-            asked_ref[slots[m]], key_ref[pages[m]], NT, preferred_element_type=F32
+            query, key_ref[pages[m]], NT, preferred_element_type=F32
         )
     scores = score_ref[...] * scale
     highest = jnp.max(scores, axis=-1, keepdims=True)
@@ -88,8 +98,10 @@
         out_ref[slots[m]] = message.astype(BF16)
 
 
-def local_kernel(scale, first, query_ref, key_ref, value_ref, table_ref, length_ref, out_ref, stat_ref, bias_ref, score_ref):
+def local_kernel(scale, first, query_ref, key_ref, value_ref, table_ref, length_ref, *rest):
+    out_ref, stat_ref, bias_ref, score_ref = rest[-4:]
     heads, requests, width = out_ref.shape
+    heads = heads - first
     pool, page_len, _ = key_ref.shape
     pairs = pool // 2
     entries = table_ref.shape[0]
@@ -122,13 +134,17 @@
         total = total + weights
         rounded = weights.astype(BF16).reshape(heads * requests, 2 * page_len)
         out = out + jnp.dot(rounded, values, preferred_element_type=F32)
-    out_ref[...] = out.reshape(heads, requests, width)
+    out_ref[first:] = out.reshape(heads, requests, width)
     total = jnp.sum(total, axis=-1, keepdims=True)
     lane = lax.broadcasted_iota(jnp.int32, (requests, LANES), 1)
     stats = jnp.zeros((requests, LANES), F32)
     for h in range(heads):
         stats = jnp.where(lane == first + h, best[h], stats)
         stats = jnp.where(lane == SLOTS + first + h, total[h], stats)
+    stats = stats.T[: 2 * SLOTS]
+    if first:
+        out_ref[:first] = rest[0][...]
+        stats = stats + rest[1][...]
     stat_ref[...] = stats
 
 
@@ -147,37 +163,39 @@
     extra_ref[...] = jnp.where(place == 0, upper, jnp.where(place == 1, lower, 0.0))
 
 
-def bits():
+def place():
     rank = lax.axis_index("tp")
-    return rank // 2 % 2, rank // 4, rank % 2
+    return rank // 4, rank % 2, rank // 2 % 2
 
 
 def first_kernel(partial_ref, extra_ref, send_ref, keep_ref):
-    near, _, _ = bits()
+    _, side, _ = place()
     rows = partial_ref.shape[1]
     for i in range(2):
         for j in range(2):
-            keep_ref[i, j, :rows] = partial_ref[4 * i + 2 * near + j]
+            keep_ref[i, j, :rows] = partial_ref[4 * i + 2 * j + side]
             keep_ref[i, j, rows:] = extra_ref[...]
-            send_ref[i, j, :rows] = partial_ref[4 * i + 2 * (1 - near) + j].astype(BF16)
+            send_ref[i, j, :rows] = partial_ref[4 * i + 2 * j + 1 - side].astype(BF16)
             send_ref[i, j, rows:] = extra_ref[...].astype(BF16)
 
 
 def second_kernel(got_ref, kept_ref, _, send_ref, keep_ref):
-    _, far, _ = bits()
+    far, _, _ = place()
     keep_ref[...] = kept_ref[far] + got_ref[far].astype(F32)
     send_ref[...] = (kept_ref[1 - far] + got_ref[1 - far].astype(F32)).astype(BF16)
 
 
-def third_kernel(got_ref, keep_ref, _, send_ref, last_ref):
-    mid = bits()[2]
-    last_ref[...] = keep_ref[mid] + got_ref[mid].astype(F32)
-    send_ref[...] = (keep_ref[1 - mid] + got_ref[1 - mid].astype(F32)).astype(BF16)
-
-
-def fresh_kernel(scale, features, got_ref, last_ref, cos_ref, sin_ref, query_ref, out_a_ref, stat_a_ref, out_b_ref, stat_b_ref, kv_ref, new_out_ref, new_stat_ref):
+def third_kernel(got_ref, kept_ref, length_ref, frequency_ref, send_ref, last_ref, angle_ref):
+    _, _, near = place()
+    last_ref[...] = kept_ref[near] + got_ref[near].astype(F32)
+    send_ref[...] = (kept_ref[1 - near] + got_ref[1 - near].astype(F32)).astype(BF16)
+    requests, half = angle_ref.shape
+    lengths = jnp.broadcast_to(length_ref[...].astype(F32), (LANES, requests)).T
+    angle_ref[...] = lengths[:, :half] * frequency_ref[...]
+
+
+def fresh_kernel(scale, features, got_ref, last_ref, cos_ref, sin_ref, query_ref, kv_ref, value_ref, score_ref):
     heads, requests, width = query_ref.shape
-    part = out_a_ref.shape[0]
     total = last_ref[...] + got_ref[...].astype(F32)
     extra = jnp.sum(total[requests:], axis=0, keepdims=True)
     squares = extra[:, :LANES] + extra[:, LANES:]
@@ -189,58 +207,62 @@
     key = projected[:, :width]
     key = key * cos_ref[...] + pltpu.roll(key, width // 2, 1) * sin_ref[...]
     key = key.astype(BF16)
+    kv_ref[:, :width] = key
     value = projected[:, width:].astype(BF16)
-    kv_ref[:, :width] = key
     kv_ref[:, width:] = value
+    value_ref[...] = value.astype(F32)
     key = key.astype(F32)
-    value = value.astype(F32)
-    stats = stat_a_ref[...] + stat_b_ref[...]
-    new_stats = jnp.zeros((requests, LANES), F32)
+    scores = jnp.zeros((requests, LANES), F32)
     for h in range(heads):
-        score = jnp.sum(query_ref[h].astype(F32) * key, axis=1, keepdims=True) * scale
-        highest = stats[:, h : h + 1]
-        best = jnp.maximum(highest, score)
-        factor = jnp.exp2(highest - best)
-        fresh = jnp.exp2(score - best)
-        out = out_a_ref[h] if h < part else out_b_ref[h - part]
-        new_out_ref[h] = out * factor + fresh * value
-        sums = stats[:, SLOTS + h : SLOTS + h + 1] * factor + fresh
-        new_stats = jnp.where(lane == h, best, new_stats)
-        new_stats = jnp.where(lane == SLOTS + h, sums, new_stats)
-    new_stat_ref[...] = new_stats
+        score = jnp.sum(query_ref[h].astype(F32) * key, axis=1, keepdims=True)
+        scores = jnp.where(lane == h, score * scale, scores)
+    score_ref[...] = scores.T[:SLOTS]
 
 
 def owner_kernel(label_ref, owner_ref):
-    requests, slots = owner_ref.shape
-    labels = label_ref[...].reshape(slots, LANES).T
+    slots, requests = owner_ref.shape
+    labels = label_ref[...].reshape(slots, LANES)
     owner_ref[...] = jnp.where(
-        labels == lax.broadcasted_iota(jnp.int32, (requests, slots), 0), 0.0, FLOOR
+        labels == lax.broadcasted_iota(jnp.int32, (slots, requests), 1), 0.0, FLOOR
     )
 
 
-def combine_kernel(message_ref, owner_ref, out_ref, stat_ref, final_ref):
+def combine_kernel(message_ref, owner_ref, out_ref, stat_ref, fresh_ref, value_ref, final_ref):
     heads, requests, width = out_ref.shape
     messages = jnp.swapaxes(message_ref[...].astype(F32), 0, 1)
-    levels = messages[heads].T
-    levels = levels[0:SLOTS] + levels[SLOTS : 2 * SLOTS] + levels[2 * SLOTS : 3 * SLOTS]
-    bias = owner_ref[...]
+    levels = messages[heads]
+    levels = levels[:, :SLOTS] + levels[:, SLOTS : 2 * SLOTS] + levels[:, 2 * SLOTS : 3 * SLOTS]
+    owner = owner_ref[...]
+    scores = [owner + levels[:, h : h + 1] for h in range(heads)]
+    rows = [jnp.max(score, axis=0, keepdims=True) for score in scores]
+    moved_best = jnp.concatenate(rows + [rows[0]] * (SLOTS - heads), axis=0)
     stats = stat_ref[...]
+    highest = stats[:SLOTS]
+    fresh = fresh_ref[...]
+    best = jnp.maximum(jnp.maximum(highest, fresh), moved_best)
+    weights = [jnp.exp2(scores[h] - best[h : h + 1]) for h in range(heads)]
+    rows = [jnp.sum(weight, axis=0, keepdims=True) for weight in weights]
+    moved_sums = jnp.concatenate(rows + [rows[0]] * (SLOTS - heads), axis=0)
+    factor = jnp.exp2(highest - best)
+    fresh = jnp.exp2(fresh - best)
+    inverse = 1.0 / (stats[SLOTS:] * factor + fresh + moved_sums)
+    columns = jnp.concatenate(
+        [factor * inverse, fresh * inverse, jnp.zeros((LANES - 2 * SLOTS, requests), F32)], axis=0
+    ).T
+    value = value_ref[...]
     for h in range(heads):
-        scores = bias + levels[h : h + 1]
-        highest = stats[:, h : h + 1]
-        best = jnp.maximum(highest, jnp.max(scores, axis=1, keepdims=True))
-        weights = jnp.exp2(scores - best)
-        factor = jnp.exp2(highest - best)
-        sums = stats[:, SLOTS + h : SLOTS + h + 1] * factor + jnp.sum(weights, axis=1, keepdims=True)
-        coarse = weights.astype(BF16)
-        fine = (weights - coarse.astype(F32)).astype(BF16)
+        weight = weights[h] * inverse[h : h + 1]
+        coarse = weight.astype(BF16)
+        fine = (weight - coarse.astype(F32)).astype(BF16)
         moved = messages[h].astype(BF16)
-        total = (
-            out_ref[h] * factor
-            + jnp.dot(coarse, moved, preferred_element_type=F32)
-            + jnp.dot(fine, moved, preferred_element_type=F32)
+        total = lax.dot_general(
+            jnp.concatenate([coarse, fine], axis=0),
+            jnp.concatenate([moved, moved], axis=0),
+            TN,
+            preferred_element_type=F32,
         )
-        final_ref[:, h * width : (h + 1) * width] = (total / sums).astype(BF16)
+        total = total + out_ref[h] * columns[:, h : h + 1] + value * columns[:, SLOTS + h : SLOTS + h + 1]
+        final_ref[:, h * width : (h + 1) * width] = total.astype(BF16)
 
 
 def call(kernel, shapes, ins, scratch=(), limit=8, flops=10**9, moved=0):
@@ -255,13 +277,9 @@
     )
 
 
-def rotation(lengths, width):
+def frequencies(width):
     steps = jnp.arange(width // 2, dtype=F32)
-    frequency = ROPE_BASE ** (-2.0 * steps / width)
-    angles = lengths.astype(F32)[:, None] * frequency[None, :]
-    cosine = jnp.cos(angles)
-    sine = jnp.sin(angles)
-    return jnp.concatenate([cosine, cosine], axis=1), jnp.concatenate([-sine, sine], axis=1)
+    return (ROPE_BASE ** (-2.0 * steps / width))[None, :]
 
 
 def body(
@@ -304,9 +322,9 @@
     labels = call(
         functools.partial(label_kernel, bits, root),
         shape((instances, 1, LANES), jnp.int32),
-        [SMEM],
+        [VMEM],
         flops=10**10,
-    )(plan)
+    )(plan.reshape(1, moves))
     labels = exchange(labels)
 
     scaled, extra = call(
@@ -321,63 +339,67 @@
         [shape((2, 2, padded, 2 * width), BF16), shape((2, 2, padded, 2 * width), F32)],
         [VMEM, VMEM],
     )(partial, extra)
-    got = swap(send, 2)
-
-    def local(first, count, weight):
+    got = swap(send, 1)
+
+    def local(first, stop, cost, *earlier):
         return call(
             functools.partial(local_kernel, scale, first),
-            [shape((count, requests, width), F32), shape((requests, LANES), F32)],
-            [VMEM] * 5,
+            [shape((stop, requests, width), F32), shape((2 * SLOTS, requests), F32)],
+            [VMEM] * 5 + [VMEM, VMEM, ANY][: len(earlier)],
             [
                 pltpu.VMEM((pool // 2, requests, 2 * page_len), F32),
-                pltpu.VMEM((pool // 2, count, requests, 2 * page_len), F32),
+                pltpu.VMEM((pool // 2, stop - first, requests, 2 * page_len), F32),
             ],
             limit=16,
-            flops=4 * weight * count * requests * pool * page_len * width,
-            moved=4 * pool * page_len * width,
-        )(by_head, keys, values, page_table.T, lengths[None, :])
-
-    asked = call(ask_kernel, shape((instances, SLOTS, width), BF16), [VMEM, VMEM, ANY])(labels, by_head, send)
+            flops=cost,
+        )(by_head, keys, values, page_table.T, lengths[None, :], *earlier)
+
+    asked = call(ask_kernel, shape((instances, 2, heads // 2 * width), BF16), [VMEM, VMEM, ANY])(labels, by_head, send)
     asked = exchange(asked)
 
-    out_a, stat_a = local(0, heads // 2, 12)
+    out, stats = local(0, heads // 2, 3 * 10**9)
     send, keep = call(
         second_kernel,
         [shape((2, padded, 2 * width), BF16), shape((2, padded, 2 * width), F32)],
         [VMEM, VMEM, ANY],
-    )(got, keep, stat_a)
+        flops=SECOND,
+    )(got, keep, stats)
     got = swap(send, 4)
 
     answers = call(
         functools.partial(moved_kernel, scale, heads, bits, root),
         shape((instances, SLOTS, width), BF16),
-        [SMEM, VMEM, VMEM, VMEM, ANY],
+        [VMEM, VMEM, VMEM, VMEM, ANY],
         [pltpu.VMEM((moves, SLOTS, page_len), F32)],
-    )(plan, asked, keys, values, send)
+    )(plan.reshape(1, moves), asked, keys, values, send)
     answers = exchange(answers)
 
     owner = call(
-        owner_kernel, shape((requests, instances), F32), [VMEM], flops=WAIT
+        owner_kernel, shape((instances, requests), F32), [VMEM], flops=0
     )(labels)
-    out_b, stat_b = local(heads // 2, heads - heads // 2, 1)
-    send, last = call(
+    send, last, angles = call(
         third_kernel,
-        [shape((padded, 2 * width), BF16), shape((padded, 2 * width), F32)],
-        [VMEM, VMEM, ANY],
-    )(got, keep, owner)
-    got = swap(send, 1)
-    cosine, sine = rotation(lengths, width)
-    new_kv, out, stats = call(
+        [
+            shape((padded, 2 * width), BF16),
+            shape((padded, 2 * width), F32),
+            shape((requests, width // 2), F32),
+        ],
+        [VMEM] * 4,
+        flops=THIRD,
+    )(got, keep, lengths[None, :], frequencies(width))
+    out, stats = local(heads // 2, heads, LATER, out, stats, send)
+    got = swap(send, 2)
+    cosine = jnp.cos(angles)
+    sine = jnp.sin(angles)
+    cosine = jnp.concatenate([cosine, cosine], axis=1)
+    sine = jnp.concatenate([-sine, sine], axis=1)
+    new_kv, value, fresh = call(
         functools.partial(fresh_kernel, scale, features),
-        [
-            shape((requests, 2 * width), BF16),
-            shape((heads, requests, width), F32),
-            shape((requests, LANES), F32),
-        ],
-        [VMEM] * 9,
-    )(got, last, cosine, sine, by_head, out_a, stat_a, out_b, stat_b)
-    attention_out = call(combine_kernel, shape((requests, heads * width), BF16), [VMEM] * 4)(
-        answers, owner, out, stats
+        [shape((requests, 2 * width), BF16), shape((requests, width), F32), shape((SLOTS, requests), F32)],
+        [VMEM] * 5,
+    )(got, last, cosine, sine, by_head)
+    attention_out = call(combine_kernel, shape((requests, heads * width), BF16), [VMEM] * 6)(
+        answers, owner, out, stats, fresh, value
     )
     return (attention_out, new_kv.reshape(requests, 1, 2 * width))
 

time: 79.4 us -> 75.8 us (0.955)
  Pallas kernels: 15 us -> 11.5 us
  waiting for transfers between devices: 0.02 us -> 1.3 us
  other arithmetic: 1.76 us -> 0.82 us
    all_to_all x3, waiting for transfers between devices: 0.01 us -> 1.29 us  [exchange(): lax.all_to_all(x, 'inst', 0, 0, tiled=True, axis_index_groups=[order])]
    pallas_call x1, Pallas kernels: 2.16 us -> 0.89 us  [body(): call(functools.partial(fresh_kernel, scale, features), [shape((requests,...]
    pallas_call x5, Pallas kernels: 9.06 us -> 7.81 us  [the longest x2 5.55 us: local(): call(functools.partial(local_kernel, scale, first), [shape((stop, request...]
    neg x1, other arithmetic: 0.95 us -> 0.01 us  [body(): sine = jnp.concatenate([-sine, sine], axis=1)]
  transfers between devices with their start and end apart: 6 -> 6, of which waited for: 0 -> 1; matrix products, arithmetic and copies ran while one was open for 2% -> 1% of each run, Pallas kernels for 14% -> 13%
where the time goes in v2:
time: 75.8 us; the launch traced here: 75.5 us
  starting transfers between devices  60 us (79%)
  Pallas kernels  11.5 us (15%)
  waiting for transfers between devices  1.3 us (2%)
  between operations  0.89 us (1%)
  other arithmetic  0.82 us (1%)
    all_to_all x3, starting transfers between devices, exchange(): lax.all_to_all(x, 'inst', 0, 0, tiled=True, axis_index_groups=[order])  48.3 us
    ppermute x3, starting transfers between devices, swap(): return lax.ppermute(x, 'tp', [(i, i ^ bit) for i in range(ranks)])  11.7 us
    pallas_call x2, Pallas kernels, local(): call(functools.partial(local_kernel, scale, first), [shape((stop, request...  5.55 us
    pallas_call x1, Pallas kernels, body(): call(functools.partial(moved_kernel, scale, heads, bits, root), shape((in...  1.71 us
  transfers between devices with their start and end apart: 6, of which 1 were waited for; matrix products, arithmetic and copies ran while one was open for 1% of the time, Pallas kernels for 13%

profile of v2, /device:TPU:1, one launch (start us, length us, event | category | flops | bytes accessed | tf_op | source)
XLA Modules:
  0.0 75.5 jit_solution(10352450259011396260)
XLA Ops:
  0.6 0.7 fusion.8.plan_ref
  1.3 0.7 shard_map.122
  2.1 20.8 %all-to-all-start = ((s32[64,1,128]{2,1,0:T(1,128)}), s32[64,1,128]{2,1,0:T(1,128)S(1)}, u32[]{:S(2)}, u32[]{:S(2)}) async-start(s32[64,1,128]{2,1,0:T(1,128)} %shard_map.122), calls=%async_computation | async-start | bytes 65536 | tf_op jit(solution)/shard_map/all_to_all | solution.py:310
  22.9 0.0 copy-done
  22.9 0.2 shard_map.123
  23.1 0.7 fusion.2.partial_ref
  23.7 0.0 copy-start.1
  23.7 0.0 copy-start.2
  23.8 0.0 copy-start.4
  23.8 0.0 copy-start.5
  23.8 0.1 shard_map.124
  23.9 4.8 %collective-permute-start = (bf16[2,2,144,256]{3,2,1,0:T(8,128)(2,1)S(1)}, bf16[2,2,144,256]{3,2,1,0:T(8,128)(2,1)S(1)}, u32[]{:S(2)}, u32[]{:S(2)}) collective-permute-start(bf16[2,2,144,256]{3,2,1,0:T(8,128)(2,1)S(1)} %get-tuple-element.20.rest_0_), channel_id=1, source_target_pairs={{0,1},{1,0},{2,3},{3,2},{4,5},{5,4},{6,7},{7,6},{8,9},{9,8},{10,11... | collective-permute-start | bytes 884744 | tf_op jit(solution)/shard_map/ppermute | solution.py:314
  28.7 0.0 all-to-all-done.label_ref
  28.7 0.9 %shard_map.125 = bf16[64,2,384]{2,1,0:T(2,128)(2,1)} custom-call(s32[64,1,128]{2,1,0:T(1,128)S(1)} %all-to-all-done.label_ref, bf16[6,128,128]{2,1,0:T(8,128)(2,1)S(1)} %bitcast.27, bf16[2,2,144,256]{3,2,1,0:T(8,128)(2,1)S(1)} %get-tuple-element.20.rest_0_), custom_call_target="tpu_custom_call" | custom-call | flops 1000000000 | tf_op jit(solution)/shard_map/pallas_call | solution.py:357
  29.6 13.8 %all-to-all-start.1 = ((bf16[64,2,384]{2,1,0:T(2,128)(2,1)}), bf16[64,2,384]{2,1,0:T(2,128)(2,1)S(1)}, u32[]{:S(2)}, u32[]{:S(2)}) async-start(bf16[64,2,384]{2,1,0:T(2,128)(2,1)} %shard_map.125), calls=%async_computation.1 | async-start | bytes 196608 | tf_op jit(solution)/shard_map/all_to_all | solution.py:310
  43.4 2.8 %shard_map.126 = (f32[3,128,128]{2,1,0:T(8,128)S(1)}, f32[16,128]{1,0:T(8,128)S(1)}) custom-call(bf16[6,128,128]{2,1,0:T(8,128)(2,1)S(1)} %bitcast.28, bf16[20,128,128]{2,1,0:T(8,128)(2,1)S(1)} %bitcast.21, bf16[20,128,128]{2,1,0:T(8,128)(2,1)S(1)} %bitcast.24, s32[12,128]{1,0:T(8,128)S(1)} %bitcast.31, s32[1,128]{1,0:T(1,128)S(1)} %bitcast.33), custom_call_target="tpu_custom_call" | custom-call | flops 3000000000 | tf_op jit(solution)/shard_map/pallas_call | solution.py:345
  46.2 0.0 collective-permute-done.got_ref
  46.2 0.1 shard_map.127
  46.3 4.7 %collective-permute-start.1 = (bf16[2,144,256]{2,1,0:T(8,128)(2,1)S(1)}, bf16[2,144,256]{2,1,0:T(8,128)(2,1)S(1)}, u32[]{:S(2)}, u32[]{:S(2)}) collective-permute-start(bf16[2,144,256]{2,1,0:T(8,128)(2,1)S(1)} %get-tuple-element.23.rest_0_), channel_id=1, source_target_pairs={{0,4},{1,5},{2,6},{3,7},{4,0},{5,1},{6,2},{7,3},{8,12},{9,13},{10,... | collective-permute-start | bytes 442376 | tf_op jit(solution)/shard_map/ppermute | solution.py:314
  51.0 0.0 all-to-all-done.1.asked_ref
  51.0 1.7 %shard_map.128 = bf16[64,8,128]{2,1,0:T(8,128)(2,1)} custom-call(s32[1,32]{1,0:T(1,128)S(1)} %fusion.8.plan_ref, bf16[64,2,384]{2,1,0:T(2,128)(2,1)S(1)} %all-to-all-done.1.asked_ref, bf16[20,128,128]{2,1,0:T(8,128)(2,1)S(1)} %bitcast.22, bf16[20,128,128]{2,1,0:T(8,128)(2,1)S(1)} %bitcast.25, bf16[2,144,256]{2,1,0:T(8,128)(2,1)S(1)} %get-tuple-element.23.rest_0_), custom_call_target="tpu_custom_call" | custom-call | flops 1000000000 | tf_op jit(solution)/shard_map/pallas_call | solution.py:369
  52.7 13.8 %all-to-all-start.2 = ((bf16[64,8,128]{2,1,0:T(8,128)(2,1)}), bf16[64,8,128]{2,1,0:T(8,128)(2,1)S(1)}, u32[]{:S(2)}, u32[]{:S(2)}) async-start(bf16[64,8,128]{2,1,0:T(8,128)(2,1)} %shard_map.128), calls=%async_computation.2 | async-start | bytes 262144 | tf_op jit(solution)/shard_map/all_to_all | solution.py:310
  66.5 0.0 collective-permute-done.1.got_ref
  66.5 0.1 shard_map.130
  66.6 2.2 %collective-permute-start.2 = (bf16[144,256]{1,0:T(8,128)(2,1)S(1)}, bf16[144,256]{1,0:T(8,128)(2,1)S(1)}, u32[]{:S(2)}, u32[]{:S(2)}) collective-permute-start(bf16[144,256]{1,0:T(8,128)(2,1)S(1)} %get-tuple-element.26.rest_2_), channel_id=1, source_target_pairs={{0,2},{1,3},{2,0},{3,1},{4,6},{5,7},{6,4},{7,5},{8,10},{9,11},{10,... | collective-permute-start | bytes 221192 | tf_op jit(solution)/shard_map/ppermute | solution.py:314
  68.8 0.2 fusion.9
  69.1 2.8 %shard_map.131 = (f32[6,128,128]{2,1,0:T(8,128)S(1)}, f32[16,128]{1,0:T(8,128)S(1)}) custom-call(bf16[6,128,128]{2,1,0:T(8,128)(2,1)S(1)} %bitcast.29, bf16[20,128,128]{2,1,0:T(8,128)(2,1)S(1)} %bitcast.23, bf16[20,128,128]{2,1,0:T(8,128)(2,1)S(1)} %bitcast.26, s32[12,128]{1,0:T(8,128)S(1)} %bitcast.32, s32[1,128]{1,0:T(1,128)S(1)} %bitcast.35, ...), custom_call_target="tpu_custom_call" | custom-call | flops 200000000 | tf_op jit(solution)/shard_map/pallas_call | solution.py:345
  71.9 0.1 pad_maximum_fusion
  72.0 0.0 collective-permute-done.2.got_ref
  72.0 0.9 %shard_map.132 = (bf16[128,256]{1,0:T(8,128)(2,1)}, f32[128,128]{1,0:T(8,128)S(1)}, f32[8,128]{1,0:T(8,128)S(1)}) custom-call(bf16[144,256]{1,0:T(8,128)(2,1)S(1)} %collective-permute-done.2.got_ref, f32[144,256]{1,0:T(8,128)S(1)} %get-tuple-element.29.last_ref, f32[128,128]{1,0:T(8,128)S(1)} %get-tuple-element.36.cos_ref, ...), custom_call_target="tpu_custom_call" | custom-call | flops 1000000000 | tf_op jit(solution)/shard_map/pallas_call | solution.py:396
  72.9 1.3 %all-to-all-done.2.message_ref = bf16[64,8,128]{2,1,0:T(8,128)(2,1)S(1)} async-done(((bf16[64,8,128]{2,1,0:T(8,128)(2,1)}), bf16[64,8,128]{2,1,0:T(8,128)(2,1)S(1)}, u32[]{:S(2)}, u32[]{:S(2)}) %all-to-all-start.2) | async-done | bytes 131104 | tf_op jit(solution)/shard_map/all_to_all | solution.py:310
  74.2 1.3 %shard_map.133 = bf16[128,768]{1,0:T(8,128)(2,1)} custom-call(bf16[64,8,128]{2,1,0:T(8,128)(2,1)S(1)} %all-to-all-done.2.message_ref, f32[64,128]{1,0:T(8,128)S(1)} %shard_map.129.owner_ref, f32[6,128,128]{2,1,0:T(8,128)S(1)} %get-tuple-element.27.out_ref, f32[16,128]{1,0:T(8,128)S(1)} %get-tuple-element.28.stat_ref, ...), custom_call_target="tpu_custom_call" | custom-call | flops 1000000000 | tf_op jit(solution)/shard_map/pallas_call | solution.py:401
  (14 shorter events, 0.1 us)
Async XLA Ops:
  1.3 21.5 %copy-start = (bf16[768,8,256]{2,1,0:T(8,128)(2,1)S(1)}, bf16[768,8,256]{2,1,0:T(8,128)(2,1)}, u32[]{:S(2)}) copy-start(bf16[768,8,256]{2,1,0:T(8,128)(2,1)} %_.1) | copy-start | bytes 9437188
  1.3 21.6 %copy-start.6 = (bf16[128,768]{1,0:T(8,128)(2,1)S(1)}, bf16[128,768]{1,0:T(8,128)(2,1)}, u32[]{:S(2)}) copy-start(bf16[128,768]{1,0:T(8,128)(2,1)} %hidden_ref.1) | copy-start | bytes 589828
  1.3 21.6 %copy-start.7 = (bf16[768]{0:T(1024)(128)(2,1)S(1)}, bf16[768]{0:T(1024)(128)(2,1)}, u32[]{:S(2)}) copy-start(bf16[768]{0:T(1024)(128)(2,1)} %gain_ref.1) | copy-start | bytes 4612
  2.1 26.6 %all-to-all-start = ((s32[64,1,128]{2,1,0:T(1,128)}), s32[64,1,128]{2,1,0:T(1,128)S(1)}, u32[]{:S(2)}, u32[]{:S(2)}) async-start(s32[64,1,128]{2,1,0:T(1,128)} %shard_map.122), calls=%async_computation | async-start | bytes 65536 | tf_op jit(solution)/shard_map/all_to_all | solution.py:310
  23.1 5.7 %copy-start.3 = (bf16[128,6,128]{2,0,1:T(8,128)(2,1)S(1)}, bf16[128,6,128]{2,0,1:T(8,128)(2,1)}, u32[]{:S(2)}) copy-start(bf16[128,6,128]{2,0,1:T(8,128)(2,1)} %param.14) | copy-start | bytes 589828
  23.7 19.7 %copy-start.1 = (bf16[20,1,128,128]{3,2,1,0:T(8,128)(2,1)S(1)}, bf16[20,1,128,128]{3,2,1,0:T(8,128)(2,1)}, u32[]{:S(2)}) copy-start(bf16[20,1,128,128]{3,2,1,0:T(8,128)(2,1)} %param.15) | copy-start | bytes 1966084
  23.7 19.7 %copy-start.2 = (bf16[20,1,128,128]{3,2,1,0:T(8,128)(2,1)S(1)}, bf16[20,1,128,128]{3,2,1,0:T(8,128)(2,1)}, u32[]{:S(2)}) copy-start(bf16[20,1,128,128]{3,2,1,0:T(8,128)(2,1)} %param.16) | copy-start | bytes 1966084
  23.8 19.7 %copy-start.4 = (s32[128,12]{0,1:T(8,128)S(1)}, s32[128,12]{0,1:T(8,128)}, u32[]{:S(2)}) copy-start(s32[128,12]{0,1:T(8,128)} %param.17) | copy-start | bytes 18436
  23.8 19.6 %copy-start.5 = (s32[128]{0:T(128)S(1)}, s32[128]{0:T(128)}, u32[]{:S(2)}) copy-start(s32[128]{0:T(128)} %param.18) | copy-start | bytes 1540
  23.9 22.3 %collective-permute-start = (bf16[2,2,144,256]{3,2,1,0:T(8,128)(2,1)S(1)}, bf16[2,2,144,256]{3,2,1,0:T(8,128)(2,1)S(1)}, u32[]{:S(2)}, u32[]{:S(2)}) collective-permute-start(bf16[2,2,144,256]{3,2,1,0:T(8,128)(2,1)S(1)} %get-tuple-element.20.rest_0_), channel_id=1, source_target_pairs={{0,1},{1,0},{2,3},{3,2},{4,5},{5,4},{6,7},{7,6},{8,9},{9,8},{10,11... | collective-permute-start | bytes 884744 | tf_op jit(solution)/shard_map/ppermute | solution.py:314
  29.6 21.4 %all-to-all-start.1 = ((bf16[64,2,384]{2,1,0:T(2,128)(2,1)}), bf16[64,2,384]{2,1,0:T(2,128)(2,1)S(1)}, u32[]{:S(2)}, u32[]{:S(2)}) async-start(bf16[64,2,384]{2,1,0:T(2,128)(2,1)} %shard_map.125), calls=%async_computation.1 | async-start | bytes 196608 | tf_op jit(solution)/shard_map/all_to_all | solution.py:310
  46.3 20.2 %collective-permute-start.1 = (bf16[2,144,256]{2,1,0:T(8,128)(2,1)S(1)}, bf16[2,144,256]{2,1,0:T(8,128)(2,1)S(1)}, u32[]{:S(2)}, u32[]{:S(2)}) collective-permute-start(bf16[2,144,256]{2,1,0:T(8,128)(2,1)S(1)} %get-tuple-element.23.rest_0_), channel_id=1, source_target_pairs={{0,4},{1,5},{2,6},{3,7},{4,0},{5,1},{6,2},{7,3},{8,12},{9,13},{10,... | collective-permute-start | bytes 442376 | tf_op jit(solution)/shard_map/ppermute | solution.py:314
  52.7 21.4 %all-to-all-start.2 = ((bf16[64,8,128]{2,1,0:T(8,128)(2,1)}), bf16[64,8,128]{2,1,0:T(8,128)(2,1)S(1)}, u32[]{:S(2)}, u32[]{:S(2)}) async-start(bf16[64,8,128]{2,1,0:T(8,128)(2,1)} %shard_map.128), calls=%async_computation.2 | async-start | bytes 262144 | tf_op jit(solution)/shard_map/all_to_all | solution.py:310
  66.6 5.4 %collective-permute-start.2 = (bf16[144,256]{1,0:T(8,128)(2,1)S(1)}, bf16[144,256]{1,0:T(8,128)(2,1)S(1)}, u32[]{:S(2)}, u32[]{:S(2)}) collective-permute-start(bf16[144,256]{1,0:T(8,128)(2,1)S(1)} %get-tuple-element.26.rest_2_), channel_id=1, source_target_pairs={{0,2},{1,3},{2,0},{3,1},{4,6},{5,7},{6,4},{7,5},{8,10},{9,11},{10,... | collective-permute-start | bytes 221192 | tf_op jit(solution)/shard_map/ppermute | solution.py:314

commit v3 on v2

--- a/solution.py
+++ b/solution.py
@@ -99,53 +99,49 @@
 
 
 def local_kernel(scale, first, query_ref, key_ref, value_ref, table_ref, length_ref, *rest):
-    out_ref, stat_ref, bias_ref, score_ref = rest[-4:]
+    out_ref, stat_ref, score_ref = rest[-3:]
     heads, requests, width = out_ref.shape
     heads = heads - first
     pool, page_len, _ = key_ref.shape
     pairs = pool // 2
-    entries = table_ref.shape[0]
+    span = 2 * page_len
     lengths = length_ref[...]
-    page = lax.broadcasted_iota(jnp.int32, (LANES, requests), 0)
-    counts = jnp.zeros((LANES, requests), jnp.int32)
-    for i in range(entries):
+    page = lax.broadcasted_iota(jnp.int32, (pool, requests), 0)
+    counts = jnp.zeros((pool, requests), jnp.int32)
+    for i in range(table_ref.shape[0]):
         held = jnp.clip(lengths - i * page_len, 0, page_len)
         counts = counts + jnp.where(table_ref[i : i + 1, :] == page, held, 0)
-    counts = counts.astype(F32).T
-    token = lax.broadcasted_iota(jnp.int32, (requests, page_len), 1).astype(F32)
-    for p in range(pool):
-        bias_ref[p // 2, :, (p % 2) * page_len : (p % 2 + 1) * page_len] = jnp.where(
-            token < counts[:, p : p + 1], 0.0, FLOOR
-        )
+    token = lax.broadcasted_iota(jnp.int32, (page_len, requests), 0)
     query = query_ref[first : first + heads].reshape(heads * requests, width)
-    best = jnp.full((heads, requests, 2 * page_len), FLOOR, F32)
+    lanes = [slice(h * requests, (h + 1) * requests) for h in range(heads)]
+    best = [jnp.full((8, requests), FLOOR, F32)] * heads
     for p in range(pairs):
-        keys = key_ref[2 * p : 2 * p + 2].reshape(2 * page_len, width)
-        scores = lax.dot_general(query, keys, NT, preferred_element_type=F32)
-        scores = scores.reshape(heads, requests, 2 * page_len) * scale + bias_ref[p][None]
-        score_ref[p] = scores
-        best = jnp.maximum(best, scores)
-    best = jnp.max(best, axis=-1, keepdims=True)
-    total = jnp.zeros((heads, requests, 2 * page_len), F32)
-    out = jnp.zeros((heads * requests, width), F32)
+        keys = key_ref[2 * p : 2 * p + 2].reshape(span, width)
+        scores = lax.dot_general(keys, query, NT, preferred_element_type=F32)
+        usable = [token < counts[2 * p + i : 2 * p + i + 1] for i in range(2)]
+        usable = jnp.concatenate(usable, axis=0)
+        for h in range(heads):
+            masked = jnp.where(usable, scores[:, lanes[h]] * scale, FLOOR)
+            score_ref[p, :, lanes[h]] = masked
+            best[h] = jnp.maximum(best[h], jnp.max(masked.reshape(span // 8, 8, requests), axis=0))
+    best = jnp.concatenate([jnp.max(b, axis=0, keepdims=True) for b in best], axis=1)
+    total = jnp.zeros((8, heads * requests), F32)
+    out = jnp.zeros((width, heads * requests), F32)
     for p in range(pairs):
-        values = value_ref[2 * p : 2 * p + 2].reshape(2 * page_len, width)
         weights = jnp.exp2(score_ref[p] - best)
-        total = total + weights
-        rounded = weights.astype(BF16).reshape(heads * requests, 2 * page_len)
-        out = out + jnp.dot(rounded, values, preferred_element_type=F32)
-    out_ref[first:] = out.reshape(heads, requests, width)
-    total = jnp.sum(total, axis=-1, keepdims=True)
-    lane = lax.broadcasted_iota(jnp.int32, (requests, LANES), 1)
-    stats = jnp.zeros((requests, LANES), F32)
-    for h in range(heads):
-        stats = jnp.where(lane == first + h, best[h], stats)
-        stats = jnp.where(lane == SLOTS + first + h, total[h], stats)
-    stats = stats.T[: 2 * SLOTS]
+        total = total + jnp.sum(weights.reshape(span // 8, 8, heads * requests), axis=0)
+        values = value_ref[2 * p : 2 * p + 2].reshape(span, width)
+        out = out + lax.dot_general(values, weights.astype(BF16), TN, preferred_element_type=F32)
+    total = jnp.sum(total, axis=0, keepdims=True)
     if first:
         out_ref[:first] = rest[0][...]
-        stats = stats + rest[1][...]
-    stat_ref[...] = stats
+        stat_ref[...] = rest[1][...]
+    else:
+        stat_ref[...] = jnp.zeros(stat_ref.shape, F32)
+    for h in range(heads):
+        out_ref[first + h] = out[:, lanes[h]].T
+        stat_ref[first + h : first + h + 1] = best[:, lanes[h]]
+        stat_ref[SLOTS + first + h : SLOTS + first + h + 1] = total[:, lanes[h]]
 
 
 def norm_kernel(hidden_ref, gain_ref, _, scaled_ref, extra_ref):
@@ -169,13 +165,13 @@
 
 
 def first_kernel(partial_ref, extra_ref, send_ref, keep_ref):
-    _, side, _ = place()
+    _, _, near = place()
     rows = partial_ref.shape[1]
     for i in range(2):
         for j in range(2):
-            keep_ref[i, j, :rows] = partial_ref[4 * i + 2 * j + side]
+            keep_ref[i, j, :rows] = partial_ref[4 * i + 2 * near + j]
             keep_ref[i, j, rows:] = extra_ref[...]
-            send_ref[i, j, :rows] = partial_ref[4 * i + 2 * j + 1 - side].astype(BF16)
+            send_ref[i, j, :rows] = partial_ref[4 * i + 2 * (1 - near) + j].astype(BF16)
             send_ref[i, j, rows:] = extra_ref[...].astype(BF16)
 
 
@@ -186,15 +182,15 @@
 
 
 def third_kernel(got_ref, kept_ref, length_ref, frequency_ref, send_ref, last_ref, angle_ref):
-    _, _, near = place()
-    last_ref[...] = kept_ref[near] + got_ref[near].astype(F32)
-    send_ref[...] = (kept_ref[1 - near] + got_ref[1 - near].astype(F32)).astype(BF16)
+    _, side, _ = place()
+    last_ref[...] = kept_ref[side] + got_ref[side].astype(F32)
+    send_ref[...] = (kept_ref[1 - side] + got_ref[1 - side].astype(F32)).astype(BF16)
     requests, half = angle_ref.shape
     lengths = jnp.broadcast_to(length_ref[...].astype(F32), (LANES, requests)).T
     angle_ref[...] = lengths[:, :half] * frequency_ref[...]
 
 
-def fresh_kernel(scale, features, got_ref, last_ref, cos_ref, sin_ref, query_ref, kv_ref, value_ref, score_ref):
+def fresh_kernel(scale, features, got_ref, last_ref, cos_ref, sin_ref, query_ref, kv_ref, score_ref):
     heads, requests, width = query_ref.shape
     total = last_ref[...] + got_ref[...].astype(F32)
     extra = jnp.sum(total[requests:], axis=0, keepdims=True)
@@ -208,9 +204,7 @@
     key = key * cos_ref[...] + pltpu.roll(key, width // 2, 1) * sin_ref[...]
     key = key.astype(BF16)
     kv_ref[:, :width] = key
-    value = projected[:, width:].astype(BF16)
-    kv_ref[:, width:] = value
-    value_ref[...] = value.astype(F32)
+    kv_ref[:, width:] = projected[:, width:].astype(BF16)
     key = key.astype(F32)
     scores = jnp.zeros((requests, LANES), F32)
     for h in range(heads):
@@ -227,7 +221,7 @@
     )
 
 
-def combine_kernel(message_ref, owner_ref, out_ref, stat_ref, fresh_ref, value_ref, final_ref):
+def combine_kernel(message_ref, owner_ref, out_ref, stat_ref, fresh_ref, kv_ref, final_ref, new_kv_ref):
     heads, requests, width = out_ref.shape
     messages = jnp.swapaxes(message_ref[...].astype(F32), 0, 1)
     levels = messages[heads]
@@ -249,7 +243,8 @@
     columns = jnp.concatenate(
         [factor * inverse, fresh * inverse, jnp.zeros((LANES - 2 * SLOTS, requests), F32)], axis=0
     ).T
-    value = value_ref[...]
+    new_kv_ref[...] = kv_ref[...]
+    value = kv_ref[:, width:].astype(F32)
     for h in range(heads):
         weight = weights[h] * inverse[h : h + 1]
         coarse = weight.astype(BF16)
@@ -303,7 +298,7 @@
     ranks = lax.axis_size("tp")
     features = hidden_state.shape[1] * ranks
     scale = LOG2E / math.sqrt(width)
-    root = instances * 25 // 32
+    root = instances * 26 // 32
     order = [(i + root) % instances for i in range(instances)]
 
     def exchange(x):
@@ -339,17 +334,14 @@
         [shape((2, 2, padded, 2 * width), BF16), shape((2, 2, padded, 2 * width), F32)],
         [VMEM, VMEM],
     )(partial, extra)
-    got = swap(send, 1)
+    got = swap(send, 2)
 
     def local(first, stop, cost, *earlier):
         return call(
             functools.partial(local_kernel, scale, first),
             [shape((stop, requests, width), F32), shape((2 * SLOTS, requests), F32)],
             [VMEM] * 5 + [VMEM, VMEM, ANY][: len(earlier)],
-            [
-                pltpu.VMEM((pool // 2, requests, 2 * page_len), F32),
-                pltpu.VMEM((pool // 2, stop - first, requests, 2 * page_len), F32),
-            ],
+            [pltpu.VMEM((pool // 2, 2 * page_len, (stop - first) * requests), F32)],
             limit=16,
             flops=cost,
         )(by_head, keys, values, page_table.T, lengths[None, :], *earlier)
@@ -388,19 +380,21 @@
         flops=THIRD,
     )(got, keep, lengths[None, :], frequencies(width))
     out, stats = local(heads // 2, heads, LATER, out, stats, send)
-    got = swap(send, 2)
+    got = swap(send, 1)
     cosine = jnp.cos(angles)
     sine = jnp.sin(angles)
     cosine = jnp.concatenate([cosine, cosine], axis=1)
     sine = jnp.concatenate([-sine, sine], axis=1)
-    new_kv, value, fresh = call(
+    kv, fresh = call(
         functools.partial(fresh_kernel, scale, features),
-        [shape((requests, 2 * width), BF16), shape((requests, width), F32), shape((SLOTS, requests), F32)],
+        [shape((requests, 2 * width), BF16), shape((SLOTS, requests), F32)],
         [VMEM] * 5,
     )(got, last, cosine, sine, by_head)
-    attention_out = call(combine_kernel, shape((requests, heads * width), BF16), [VMEM] * 6)(
-        answers, owner, out, stats, fresh, value
-    )
+    attention_out, new_kv = call(
+        combine_kernel,
+        [shape((requests, heads * width), BF16), shape((requests, 2 * width), BF16)],
+        [VMEM] * 6,
+    )(answers, owner, out, stats, fresh, kv)
     return (attention_out, new_kv.reshape(requests, 1, 2 * width))
 
 

time: 75.8 us -> 73.2 us (0.966)
  Pallas kernels: 11.5 us -> 9.59 us
  starting transfers between devices: 60 us -> 59.1 us
    all_to_all x3, starting transfers between devices: 48.3 us -> 46.8 us  [exchange(): lax.all_to_all(x, 'inst', 0, 0, tiled=True, axis_index_groups=[order])]
    pallas_call x2, Pallas kernels: 5.55 us -> 4.08 us  [local(): call(functools.partial(local_kernel, scale, first), [shape((stop, request...]
  transfers between devices with their start and end apart: 6 -> 6, of which waited for: 1 -> 3; matrix products, arithmetic and copies ran while one was open for 1% -> 1% of each run, Pallas kernels for 13% -> 10%
where the time goes in v3:
time: 73.2 us; the launch traced here: 72.9 us
  starting transfers between devices  59.1 us (81%)
  Pallas kernels  9.59 us (13%)
  waiting for transfers between devices  1.51 us (2%)
  between operations  0.87 us (1%)
  other arithmetic  0.82 us (1%)
    all_to_all x3, starting transfers between devices, exchange(): lax.all_to_all(x, 'inst', 0, 0, tiled=True, axis_index_groups=[order])  46.8 us
    ppermute x3, starting transfers between devices, swap(): return lax.ppermute(x, 'tp', [(i, i ^ bit) for i in range(ranks)])  12.3 us
    pallas_call x2, Pallas kernels, local(): call(functools.partial(local_kernel, scale, first), [shape((stop, request...  4.08 us
    pallas_call x1, Pallas kernels, body(): call(functools.partial(moved_kernel, scale, heads, bits, root), shape((in...  1.7 us
  transfers between devices with their start and end apart: 6, of which 3 were waited for; matrix products, arithmetic and copies ran while one was open for 1% of the time, Pallas kernels for 10%

profile of v3, /device:TPU:1, one launch (start us, length us, event | category | flops | bytes accessed | tf_op | source)
XLA Modules:
  0.0 72.9 jit_solution(12450762084387267220)
XLA Ops:
  0.6 0.7 fusion.8.plan_ref
  1.3 0.7 %shard_map.122 = s32[64,1,128]{2,1,0:T(1,128)} custom-call(s32[1,32]{1,0:T(1,128)S(1)} %fusion.8.plan_ref), custom_call_target="tpu_custom_call" | custom-call | flops 10000000000 | tf_op jit(solution)/shard_map/pallas_call | solution.py:317
  2.1 19.9 %all-to-all-start = ((s32[64,1,128]{2,1,0:T(1,128)}), s32[64,1,128]{2,1,0:T(1,128)S(1)}, u32[]{:S(2)}, u32[]{:S(2)}) async-start(s32[64,1,128]{2,1,0:T(1,128)} %shard_map.122), calls=%async_computation | async-start | bytes 65536 | tf_op jit(solution)/shard_map/all_to_all | solution.py:305
  22.0 0.0 copy-done
  22.0 0.2 shard_map.123
  22.2 0.7 fusion.2.partial_ref
  22.8 0.0 copy-start.1
  22.8 0.0 copy-start.2
  22.9 0.0 copy-start.4
  22.9 0.0 copy-start.5
  22.9 0.1 shard_map.124
  23.0 3.2 %collective-permute-start = (bf16[2,2,144,256]{3,2,1,0:T(8,128)(2,1)S(1)}, bf16[2,2,144,256]{3,2,1,0:T(8,128)(2,1)S(1)}, u32[]{:S(2)}, u32[]{:S(2)}) collective-permute-start(bf16[2,2,144,256]{3,2,1,0:T(8,128)(2,1)S(1)} %get-tuple-element.21.rest_0_), channel_id=1, source_target_pairs={{0,2},{1,3},{2,0},{3,1},{4,6},{5,7},{6,4},{7,5},{8,10},{9,11},{10,... | collective-permute-start | bytes 884744 | tf_op jit(solution)/shard_map/ppermute | solution.py:309
  26.2 0.0 all-to-all-done.label_ref
  26.2 0.9 %shard_map.125 = bf16[64,2,384]{2,1,0:T(2,128)(2,1)} custom-call(s32[64,1,128]{2,1,0:T(1,128)S(1)} %all-to-all-done.label_ref, bf16[6,128,128]{2,1,0:T(8,128)(2,1)S(1)} %bitcast.27, bf16[2,2,144,256]{3,2,1,0:T(8,128)(2,1)S(1)} %get-tuple-element.21.rest_0_), custom_call_target="tpu_custom_call" | custom-call | flops 1000000000 | tf_op jit(solution)/shard_map/pallas_call | solution.py:349
  27.1 13.8 %all-to-all-start.1 = ((bf16[64,2,384]{2,1,0:T(2,128)(2,1)}), bf16[64,2,384]{2,1,0:T(2,128)(2,1)S(1)}, u32[]{:S(2)}, u32[]{:S(2)}) async-start(bf16[64,2,384]{2,1,0:T(2,128)(2,1)} %shard_map.125), calls=%async_computation.1 | async-start | bytes 196608 | tf_op jit(solution)/shard_map/all_to_all | solution.py:305
  40.9 2.0 %shard_map.126 = (f32[3,128,128]{2,1,0:T(8,128)S(1)}, f32[16,128]{1,0:T(8,128)S(1)}) custom-call(bf16[6,128,128]{2,1,0:T(8,128)(2,1)S(1)} %bitcast.28, bf16[20,128,128]{2,1,0:T(8,128)(2,1)S(1)} %bitcast.21, bf16[20,128,128]{2,1,0:T(8,128)(2,1)S(1)} %bitcast.24, s32[12,128]{1,0:T(8,128)S(1)} %bitcast.31, s32[1,128]{1,0:T(1,128)S(1)} %bitcast.33), custom_call_target="tpu_custom_call" | custom-call | flops 3000000000 | tf_op jit(solution)/shard_map/pallas_call | solution.py:340
  43.0 0.0 collective-permute-done.got_ref
  43.0 0.1 shard_map.127
  43.1 4.3 %collective-permute-start.1 = (bf16[2,144,256]{2,1,0:T(8,128)(2,1)S(1)}, bf16[2,144,256]{2,1,0:T(8,128)(2,1)S(1)}, u32[]{:S(2)}, u32[]{:S(2)}) collective-permute-start(bf16[2,144,256]{2,1,0:T(8,128)(2,1)S(1)} %get-tuple-element.24.rest_0_), channel_id=1, source_target_pairs={{0,4},{1,5},{2,6},{3,7},{4,0},{5,1},{6,2},{7,3},{8,12},{9,13},{10,... | collective-permute-start | bytes 442376 | tf_op jit(solution)/shard_map/ppermute | solution.py:309
  47.5 0.6 all-to-all-done.1.asked_ref
  48.1 1.7 %shard_map.128 = bf16[64,8,128]{2,1,0:T(8,128)(2,1)} custom-call(s32[1,32]{1,0:T(1,128)S(1)} %fusion.8.plan_ref, bf16[64,2,384]{2,1,0:T(2,128)(2,1)S(1)} %all-to-all-done.1.asked_ref, bf16[20,128,128]{2,1,0:T(8,128)(2,1)S(1)} %bitcast.22, bf16[20,128,128]{2,1,0:T(8,128)(2,1)S(1)} %bitcast.25, bf16[2,144,256]{2,1,0:T(8,128)(2,1)S(1)} %get-tuple-element.24.rest_0_), custom_call_target="tpu_custom_call" | custom-call | flops 1000000000 | tf_op jit(solution)/shard_map/pallas_call | solution.py:361
  49.8 13.2 %all-to-all-start.2 = ((bf16[64,8,128]{2,1,0:T(8,128)(2,1)}), bf16[64,8,128]{2,1,0:T(8,128)(2,1)S(1)}, u32[]{:S(2)}, u32[]{:S(2)}) async-start(bf16[64,8,128]{2,1,0:T(8,128)(2,1)} %shard_map.128), calls=%async_computation.2 | async-start | bytes 262144 | tf_op jit(solution)/shard_map/all_to_all | solution.py:305
  63.0 0.0 collective-permute-done.1.got_ref
  63.0 0.1 shard_map.130
  63.1 4.7 %collective-permute-start.2 = (bf16[144,256]{1,0:T(8,128)(2,1)S(1)}, bf16[144,256]{1,0:T(8,128)(2,1)S(1)}, u32[]{:S(2)}, u32[]{:S(2)}) collective-permute-start(bf16[144,256]{1,0:T(8,128)(2,1)S(1)} %get-tuple-element.27.rest_2_), channel_id=1, source_target_pairs={{0,1},{1,0},{2,3},{3,2},{4,5},{5,4},{6,7},{7,6},{8,9},{9,8},{10,11... | collective-permute-start | bytes 221192 | tf_op jit(solution)/shard_map/ppermute | solution.py:309
  67.8 0.2 fusion.9
  68.1 2.0 %shard_map.131 = (f32[6,128,128]{2,1,0:T(8,128)S(1)}, f32[16,128]{1,0:T(8,128)S(1)}) custom-call(bf16[6,128,128]{2,1,0:T(8,128)(2,1)S(1)} %bitcast.29, bf16[20,128,128]{2,1,0:T(8,128)(2,1)S(1)} %bitcast.23, bf16[20,128,128]{2,1,0:T(8,128)(2,1)S(1)} %bitcast.26, s32[12,128]{1,0:T(8,128)S(1)} %bitcast.32, s32[1,128]{1,0:T(1,128)S(1)} %bitcast.35, ...), custom_call_target="tpu_custom_call" | custom-call | flops 200000000 | tf_op jit(solution)/shard_map/pallas_call | solution.py:340
  70.1 0.1 pad_maximum_fusion
  70.2 0.5 collective-permute-done.2.got_ref
  70.7 0.4 shard_map.132
  71.1 0.4 all-to-all-done.2.message_ref
  71.5 1.3 %shard_map.133 = (bf16[128,768]{1,0:T(8,128)(2,1)}, bf16[128,256]{1,0:T(8,128)(2,1)}) custom-call(bf16[64,8,128]{2,1,0:T(8,128)(2,1)S(1)} %all-to-all-done.2.message_ref, f32[64,128]{1,0:T(8,128)S(1)} %shard_map.129.owner_ref, f32[6,128,128]{2,1,0:T(8,128)S(1)} %get-tuple-element.28.out_ref, f32[16,128]{1,0:T(8,128)S(1)} %get-tuple-element.29.stat_ref, ...), custom_call_target="tpu_custom_call" | custom-call | flops 1000000000 | tf_op jit(solution)/shard_map/pallas_call | solution.py:393
  (14 shorter events, 0.1 us)
Async XLA Ops:
  1.3 20.6 %copy-start = (bf16[768,8,256]{2,1,0:T(8,128)(2,1)S(1)}, bf16[768,8,256]{2,1,0:T(8,128)(2,1)}, u32[]{:S(2)}) copy-start(bf16[768,8,256]{2,1,0:T(8,128)(2,1)} %_.1) | copy-start | bytes 9437188
  1.3 20.7 %copy-start.6 = (bf16[128,768]{1,0:T(8,128)(2,1)S(1)}, bf16[128,768]{1,0:T(8,128)(2,1)}, u32[]{:S(2)}) copy-start(bf16[128,768]{1,0:T(8,128)(2,1)} %hidden_ref.1) | copy-start | bytes 589828
  1.3 20.7 %copy-start.7 = (bf16[768]{0:T(1024)(128)(2,1)S(1)}, bf16[768]{0:T(1024)(128)(2,1)}, u32[]{:S(2)}) copy-start(bf16[768]{0:T(1024)(128)(2,1)} %gain_ref.1) | copy-start | bytes 4612
  2.1 24.1 %all-to-all-start = ((s32[64,1,128]{2,1,0:T(1,128)}), s32[64,1,128]{2,1,0:T(1,128)S(1)}, u32[]{:S(2)}, u32[]{:S(2)}) async-start(s32[64,1,128]{2,1,0:T(1,128)} %shard_map.122), calls=%async_computation | async-start | bytes 65536 | tf_op jit(solution)/shard_map/all_to_all | solution.py:305
  22.2 4.1 %copy-start.3 = (bf16[128,6,128]{2,0,1:T(8,128)(2,1)S(1)}, bf16[128,6,128]{2,0,1:T(8,128)(2,1)}, u32[]{:S(2)}) copy-start(bf16[128,6,128]{2,0,1:T(8,128)(2,1)} %param.14) | copy-start | bytes 589828
  22.8 18.1 %copy-start.1 = (bf16[20,1,128,128]{3,2,1,0:T(8,128)(2,1)S(1)}, bf16[20,1,128,128]{3,2,1,0:T(8,128)(2,1)}, u32[]{:S(2)}) copy-start(bf16[20,1,128,128]{3,2,1,0:T(8,128)(2,1)} %param.15) | copy-start | bytes 1966084
  22.8 18.1 %copy-start.2 = (bf16[20,1,128,128]{3,2,1,0:T(8,128)(2,1)S(1)}, bf16[20,1,128,128]{3,2,1,0:T(8,128)(2,1)}, u32[]{:S(2)}) copy-start(bf16[20,1,128,128]{3,2,1,0:T(8,128)(2,1)} %param.16) | copy-start | bytes 1966084
  22.9 18.1 %copy-start.4 = (s32[128,12]{0,1:T(8,128)S(1)}, s32[128,12]{0,1:T(8,128)}, u32[]{:S(2)}) copy-start(s32[128,12]{0,1:T(8,128)} %param.17) | copy-start | bytes 18436
  22.9 18.1 %copy-start.5 = (s32[128]{0:T(128)S(1)}, s32[128]{0:T(128)}, u32[]{:S(2)}) copy-start(s32[128]{0:T(128)} %param.18) | copy-start | bytes 1540
  23.0 20.0 %collective-permute-start = (bf16[2,2,144,256]{3,2,1,0:T(8,128)(2,1)S(1)}, bf16[2,2,144,256]{3,2,1,0:T(8,128)(2,1)S(1)}, u32[]{:S(2)}, u32[]{:S(2)}) collective-permute-start(bf16[2,2,144,256]{3,2,1,0:T(8,128)(2,1)S(1)} %get-tuple-element.21.rest_0_), channel_id=1, source_target_pairs={{0,2},{1,3},{2,0},{3,1},{4,6},{5,7},{6,4},{7,5},{8,10},{9,11},{10,... | collective-permute-start | bytes 884744 | tf_op jit(solution)/shard_map/ppermute | solution.py:309
  27.1 20.9 %all-to-all-start.1 = ((bf16[64,2,384]{2,1,0:T(2,128)(2,1)}), bf16[64,2,384]{2,1,0:T(2,128)(2,1)S(1)}, u32[]{:S(2)}, u32[]{:S(2)}) async-start(bf16[64,2,384]{2,1,0:T(2,128)(2,1)} %shard_map.125), calls=%async_computation.1 | async-start | bytes 196608 | tf_op jit(solution)/shard_map/all_to_all | solution.py:305
  43.1 19.9 %collective-permute-start.1 = (bf16[2,144,256]{2,1,0:T(8,128)(2,1)S(1)}, bf16[2,144,256]{2,1,0:T(8,128)(2,1)S(1)}, u32[]{:S(2)}, u32[]{:S(2)}) collective-permute-start(bf16[2,144,256]{2,1,0:T(8,128)(2,1)S(1)} %get-tuple-element.24.rest_0_), channel_id=1, source_target_pairs={{0,4},{1,5},{2,6},{3,7},{4,0},{5,1},{6,2},{7,3},{8,12},{9,13},{10,... | collective-permute-start | bytes 442376 | tf_op jit(solution)/shard_map/ppermute | solution.py:309
  49.8 21.7 %all-to-all-start.2 = ((bf16[64,8,128]{2,1,0:T(8,128)(2,1)}), bf16[64,8,128]{2,1,0:T(8,128)(2,1)S(1)}, u32[]{:S(2)}, u32[]{:S(2)}) async-start(bf16[64,8,128]{2,1,0:T(8,128)(2,1)} %shard_map.128), calls=%async_computation.2 | async-start | bytes 262144 | tf_op jit(solution)/shard_map/all_to_all | solution.py:305
  63.1 7.6 %collective-permute-start.2 = (bf16[144,256]{1,0:T(8,128)(2,1)S(1)}, bf16[144,256]{1,0:T(8,128)(2,1)S(1)}, u32[]{:S(2)}, u32[]{:S(2)}) collective-permute-start(bf16[144,256]{1,0:T(8,128)(2,1)S(1)} %get-tuple-element.27.rest_2_), channel_id=1, source_target_pairs={{0,1},{1,0},{2,3},{3,2},{4,5},{5,4},{6,7},{7,6},{8,9},{9,8},{10,11... | collective-permute-start | bytes 221192 | tf_op jit(solution)/shard_map/ppermute | solution.py:309

commit v4 on v3

--- a/solution.py
+++ b/solution.py
@@ -67,14 +67,19 @@
     plan = [plan_ref[0, m] for m in range(moves)]
     slots = [slot_of(code, bits, root, out_ref.shape[0]) for code in plan]
     pages = [code & ((1 << bits[1]) - 1) for code in plan]
+    page_len = key_ref.shape[1]
+    couples = [(m, min(m + 1, moves - 1)) for m in range(0, moves, 2)]
     spare = jnp.zeros((SLOTS - heads, width), F32)
-    for m in range(moves):
-        pairs = asked_ref[slots[m]].astype(F32)
-        query = [pairs[:, i * width : (i + 1) * width] for i in range(heads // 2)]
-        query = jnp.concatenate(query + [spare], axis=0).astype(BF16)
-        score_ref[m] = lax.dot_general(
-            query, key_ref[pages[m]], NT, preferred_element_type=F32
-        )
+    for couple in couples:
+        query = []
+        for m in couple:
+            pairs = asked_ref[slots[m]].astype(F32)
+            query += [pairs[:, i * width : (i + 1) * width] for i in range(heads // 2)] + [spare]
+        query = jnp.concatenate(query, axis=0).astype(BF16)
+        keys = jnp.concatenate([key_ref[pages[m]] for m in couple], axis=0)
+        product = lax.dot_general(query, keys, NT, preferred_element_type=F32)
+        for i, m in enumerate(couple):
+            score_ref[m] = product[i * SLOTS : (i + 1) * SLOTS, i * page_len : (i + 1) * page_len]
     scores = score_ref[...] * scale
     highest = jnp.max(scores, axis=-1, keepdims=True)
     weights = jnp.exp2(scores - highest)
@@ -89,13 +94,19 @@
     part = lane // SLOTS
     stats = jnp.where(part == 0, first, jnp.where(part == 1, second, third))
     inverse = 1.0 / sums
-    rounded = weights.astype(BF16)
     out_ref[...] = jnp.zeros(out_ref.shape, out_ref.dtype)
-    for m in range(moves):
-        product = jnp.dot(rounded[m], value_ref[pages[m]], preferred_element_type=F32)
-        product = product * inverse[m]
-        message = jnp.where(row[m] < heads, product, stats[m])
-        out_ref[slots[m]] = message.astype(BF16)
+    blank = jnp.zeros((SLOTS, page_len), F32)
+    for one, other in couples:
+        spread = [
+            jnp.concatenate([weights[one], blank], axis=1),
+            jnp.concatenate([blank, weights[other]], axis=1),
+        ]
+        spread = jnp.concatenate(spread, axis=0).astype(BF16)
+        values = jnp.concatenate([value_ref[pages[one]], value_ref[pages[other]]], axis=0)
+        product = jnp.dot(spread, values, preferred_element_type=F32)
+        for i, m in enumerate((one, other)):
+            part_out = product[i * SLOTS : (i + 1) * SLOTS] * inverse[m]
+            out_ref[slots[m]] = jnp.where(row[m] < heads, part_out, stats[m]).astype(BF16)
 
 
 def local_kernel(scale, first, query_ref, key_ref, value_ref, table_ref, length_ref, *rest):

time: 73.2 us -> 72.9 us (level)
  no operation moved by 1% of the time
where the time goes in v4:
time: 72.9 us; the launch traced here: 72.5 us
  starting transfers between devices  59.1 us (81%)
  Pallas kernels  9.27 us (13%)
  waiting for transfers between devices  1.5 us (2%)
  between operations  0.87 us (1%)
  other arithmetic  0.82 us (1%)
    all_to_all x3, starting transfers between devices, exchange(): lax.all_to_all(x, 'inst', 0, 0, tiled=True, axis_index_groups=[order])  46.8 us
    ppermute x3, starting transfers between devices, swap(): return lax.ppermute(x, 'tp', [(i, i ^ bit) for i in range(ranks)])  12.3 us
    pallas_call x2, Pallas kernels, local(): call(functools.partial(local_kernel, scale, first), [shape((stop, request...  4.1 us
  transfers between devices with their start and end apart: 6, of which 3 were waited for; matrix products, arithmetic and copies ran while one was open for 1% of the time, Pallas kernels for 10%

profile of v4, /device:TPU:1, one launch (start us, length us, event | category | flops | bytes accessed | tf_op | source)
XLA Modules:
  0.0 72.5 jit_solution(9669935763067136642)
XLA Ops:
  0.6 0.7 fusion.8.plan_ref
  1.3 0.7 %shard_map.122 = s32[64,1,128]{2,1,0:T(1,128)} custom-call(s32[1,32]{1,0:T(1,128)S(1)} %fusion.8.plan_ref), custom_call_target="tpu_custom_call" | custom-call | flops 10000000000 | tf_op jit(solution)/shard_map/pallas_call | solution.py:328
  2.1 19.9 %all-to-all-start = ((s32[64,1,128]{2,1,0:T(1,128)}), s32[64,1,128]{2,1,0:T(1,128)S(1)}, u32[]{:S(2)}, u32[]{:S(2)}) async-start(s32[64,1,128]{2,1,0:T(1,128)} %shard_map.122), calls=%async_computation | async-start | bytes 65536 | tf_op jit(solution)/shard_map/all_to_all | solution.py:316
  22.0 0.0 copy-done
  22.0 0.2 shard_map.123
  22.2 0.7 fusion.2.partial_ref
  22.8 0.0 copy-start.1
  22.8 0.0 copy-start.2
  22.9 0.0 copy-start.4
  22.9 0.0 copy-start.5
  22.9 0.1 shard_map.124
  23.0 3.2 %collective-permute-start = (bf16[2,2,144,256]{3,2,1,0:T(8,128)(2,1)S(1)}, bf16[2,2,144,256]{3,2,1,0:T(8,128)(2,1)S(1)}, u32[]{:S(2)}, u32[]{:S(2)}) collective-permute-start(bf16[2,2,144,256]{3,2,1,0:T(8,128)(2,1)S(1)} %get-tuple-element.21.rest_0_), channel_id=1, source_target_pairs={{0,2},{1,3},{2,0},{3,1},{4,6},{5,7},{6,4},{7,5},{8,10},{9,11},{10,... | collective-permute-start | bytes 884744 | tf_op jit(solution)/shard_map/ppermute | solution.py:320
  26.2 0.0 all-to-all-done.label_ref
  26.2 0.9 %shard_map.125 = bf16[64,2,384]{2,1,0:T(2,128)(2,1)} custom-call(s32[64,1,128]{2,1,0:T(1,128)S(1)} %all-to-all-done.label_ref, bf16[6,128,128]{2,1,0:T(8,128)(2,1)S(1)} %bitcast.27, bf16[2,2,144,256]{3,2,1,0:T(8,128)(2,1)S(1)} %get-tuple-element.21.rest_0_), custom_call_target="tpu_custom_call" | custom-call | flops 1000000000 | tf_op jit(solution)/shard_map/pallas_call | solution.py:360
  27.1 13.8 %all-to-all-start.1 = ((bf16[64,2,384]{2,1,0:T(2,128)(2,1)}), bf16[64,2,384]{2,1,0:T(2,128)(2,1)S(1)}, u32[]{:S(2)}, u32[]{:S(2)}) async-start(bf16[64,2,384]{2,1,0:T(2,128)(2,1)} %shard_map.125), calls=%async_computation.1 | async-start | bytes 196608 | tf_op jit(solution)/shard_map/all_to_all | solution.py:316
  40.9 2.0 %shard_map.126 = (f32[3,128,128]{2,1,0:T(8,128)S(1)}, f32[16,128]{1,0:T(8,128)S(1)}) custom-call(bf16[6,128,128]{2,1,0:T(8,128)(2,1)S(1)} %bitcast.28, bf16[20,128,128]{2,1,0:T(8,128)(2,1)S(1)} %bitcast.21, bf16[20,128,128]{2,1,0:T(8,128)(2,1)S(1)} %bitcast.24, s32[12,128]{1,0:T(8,128)S(1)} %bitcast.31, s32[1,128]{1,0:T(1,128)S(1)} %bitcast.33), custom_call_target="tpu_custom_call" | custom-call | flops 3000000000 | tf_op jit(solution)/shard_map/pallas_call | solution.py:351
  43.0 0.0 collective-permute-done.got_ref
  43.0 0.1 shard_map.127
  43.1 4.3 %collective-permute-start.1 = (bf16[2,144,256]{2,1,0:T(8,128)(2,1)S(1)}, bf16[2,144,256]{2,1,0:T(8,128)(2,1)S(1)}, u32[]{:S(2)}, u32[]{:S(2)}) collective-permute-start(bf16[2,144,256]{2,1,0:T(8,128)(2,1)S(1)} %get-tuple-element.24.rest_0_), channel_id=1, source_target_pairs={{0,4},{1,5},{2,6},{3,7},{4,0},{5,1},{6,2},{7,3},{8,12},{9,13},{10,... | collective-permute-start | bytes 442376 | tf_op jit(solution)/shard_map/ppermute | solution.py:320
  47.5 0.6 all-to-all-done.1.asked_ref
  48.1 1.4 %shard_map.128 = bf16[64,8,128]{2,1,0:T(8,128)(2,1)} custom-call(s32[1,32]{1,0:T(1,128)S(1)} %fusion.8.plan_ref, bf16[64,2,384]{2,1,0:T(2,128)(2,1)S(1)} %all-to-all-done.1.asked_ref, bf16[20,128,128]{2,1,0:T(8,128)(2,1)S(1)} %bitcast.22, bf16[20,128,128]{2,1,0:T(8,128)(2,1)S(1)} %bitcast.25, bf16[2,144,256]{2,1,0:T(8,128)(2,1)S(1)} %get-tuple-element.24.rest_0_), custom_call_target="tpu_custom_call" | custom-call | flops 1000000000 | tf_op jit(solution)/shard_map/pallas_call | solution.py:372
  49.4 13.2 %all-to-all-start.2 = ((bf16[64,8,128]{2,1,0:T(8,128)(2,1)}), bf16[64,8,128]{2,1,0:T(8,128)(2,1)S(1)}, u32[]{:S(2)}, u32[]{:S(2)}) async-start(bf16[64,8,128]{2,1,0:T(8,128)(2,1)} %shard_map.128), calls=%async_computation.2 | async-start | bytes 262144 | tf_op jit(solution)/shard_map/all_to_all | solution.py:316
  62.6 0.0 collective-permute-done.1.got_ref
  62.6 0.1 shard_map.130
  62.7 4.7 %collective-permute-start.2 = (bf16[144,256]{1,0:T(8,128)(2,1)S(1)}, bf16[144,256]{1,0:T(8,128)(2,1)S(1)}, u32[]{:S(2)}, u32[]{:S(2)}) collective-permute-start(bf16[144,256]{1,0:T(8,128)(2,1)S(1)} %get-tuple-element.27.rest_2_), channel_id=1, source_target_pairs={{0,1},{1,0},{2,3},{3,2},{4,5},{5,4},{6,7},{7,6},{8,9},{9,8},{10,11... | collective-permute-start | bytes 221192 | tf_op jit(solution)/shard_map/ppermute | solution.py:320
  67.5 0.2 fusion.9
  67.7 2.0 %shard_map.131 = (f32[6,128,128]{2,1,0:T(8,128)S(1)}, f32[16,128]{1,0:T(8,128)S(1)}) custom-call(bf16[6,128,128]{2,1,0:T(8,128)(2,1)S(1)} %bitcast.29, bf16[20,128,128]{2,1,0:T(8,128)(2,1)S(1)} %bitcast.23, bf16[20,128,128]{2,1,0:T(8,128)(2,1)S(1)} %bitcast.26, s32[12,128]{1,0:T(8,128)S(1)} %bitcast.32, s32[1,128]{1,0:T(1,128)S(1)} %bitcast.35, ...), custom_call_target="tpu_custom_call" | custom-call | flops 200000000 | tf_op jit(solution)/shard_map/pallas_call | solution.py:351
  69.8 0.1 pad_maximum_fusion
  69.9 0.5 collective-permute-done.2.got_ref
  70.4 0.4 shard_map.132
  70.8 0.4 all-to-all-done.2.message_ref
  71.2 1.3 %shard_map.133 = (bf16[128,768]{1,0:T(8,128)(2,1)}, bf16[128,256]{1,0:T(8,128)(2,1)}) custom-call(bf16[64,8,128]{2,1,0:T(8,128)(2,1)S(1)} %all-to-all-done.2.message_ref, f32[64,128]{1,0:T(8,128)S(1)} %shard_map.129.owner_ref, f32[6,128,128]{2,1,0:T(8,128)S(1)} %get-tuple-element.28.out_ref, f32[16,128]{1,0:T(8,128)S(1)} %get-tuple-element.29.stat_ref, ...), custom_call_target="tpu_custom_call" | custom-call | flops 1000000000 | tf_op jit(solution)/shard_map/pallas_call | solution.py:404
  (14 shorter events, 0.1 us)
Async XLA Ops:
  1.3 20.6 %copy-start = (bf16[768,8,256]{2,1,0:T(8,128)(2,1)S(1)}, bf16[768,8,256]{2,1,0:T(8,128)(2,1)}, u32[]{:S(2)}) copy-start(bf16[768,8,256]{2,1,0:T(8,128)(2,1)} %_.1) | copy-start | bytes 9437188
  1.3 20.7 %copy-start.6 = (bf16[128,768]{1,0:T(8,128)(2,1)S(1)}, bf16[128,768]{1,0:T(8,128)(2,1)}, u32[]{:S(2)}) copy-start(bf16[128,768]{1,0:T(8,128)(2,1)} %hidden_ref.1) | copy-start | bytes 589828
  1.3 20.7 %copy-start.7 = (bf16[768]{0:T(1024)(128)(2,1)S(1)}, bf16[768]{0:T(1024)(128)(2,1)}, u32[]{:S(2)}) copy-start(bf16[768]{0:T(1024)(128)(2,1)} %gain_ref.1) | copy-start | bytes 4612
  2.1 24.1 %all-to-all-start = ((s32[64,1,128]{2,1,0:T(1,128)}), s32[64,1,128]{2,1,0:T(1,128)S(1)}, u32[]{:S(2)}, u32[]{:S(2)}) async-start(s32[64,1,128]{2,1,0:T(1,128)} %shard_map.122), calls=%async_computation | async-start | bytes 65536 | tf_op jit(solution)/shard_map/all_to_all | solution.py:316
  22.2 4.1 %copy-start.3 = (bf16[128,6,128]{2,0,1:T(8,128)(2,1)S(1)}, bf16[128,6,128]{2,0,1:T(8,128)(2,1)}, u32[]{:S(2)}) copy-start(bf16[128,6,128]{2,0,1:T(8,128)(2,1)} %param.14) | copy-start | bytes 589828
  22.8 18.1 %copy-start.1 = (bf16[20,1,128,128]{3,2,1,0:T(8,128)(2,1)S(1)}, bf16[20,1,128,128]{3,2,1,0:T(8,128)(2,1)}, u32[]{:S(2)}) copy-start(bf16[20,1,128,128]{3,2,1,0:T(8,128)(2,1)} %param.15) | copy-start | bytes 1966084
  22.8 18.1 %copy-start.2 = (bf16[20,1,128,128]{3,2,1,0:T(8,128)(2,1)S(1)}, bf16[20,1,128,128]{3,2,1,0:T(8,128)(2,1)}, u32[]{:S(2)}) copy-start(bf16[20,1,128,128]{3,2,1,0:T(8,128)(2,1)} %param.16) | copy-start | bytes 1966084
  22.9 18.1 %copy-start.4 = (s32[128,12]{0,1:T(8,128)S(1)}, s32[128,12]{0,1:T(8,128)}, u32[]{:S(2)}) copy-start(s32[128,12]{0,1:T(8,128)} %param.17) | copy-start | bytes 18436
  22.9 18.1 %copy-start.5 = (s32[128]{0:T(128)S(1)}, s32[128]{0:T(128)}, u32[]{:S(2)}) copy-start(s32[128]{0:T(128)} %param.18) | copy-start | bytes 1540
  23.0 20.0 %collective-permute-start = (bf16[2,2,144,256]{3,2,1,0:T(8,128)(2,1)S(1)}, bf16[2,2,144,256]{3,2,1,0:T(8,128)(2,1)S(1)}, u32[]{:S(2)}, u32[]{:S(2)}) collective-permute-start(bf16[2,2,144,256]{3,2,1,0:T(8,128)(2,1)S(1)} %get-tuple-element.21.rest_0_), channel_id=1, source_target_pairs={{0,2},{1,3},{2,0},{3,1},{4,6},{5,7},{6,4},{7,5},{8,10},{9,11},{10,... | collective-permute-start | bytes 884744 | tf_op jit(solution)/shard_map/ppermute | solution.py:320
  27.1 20.9 %all-to-all-start.1 = ((bf16[64,2,384]{2,1,0:T(2,128)(2,1)}), bf16[64,2,384]{2,1,0:T(2,128)(2,1)S(1)}, u32[]{:S(2)}, u32[]{:S(2)}) async-start(bf16[64,2,384]{2,1,0:T(2,128)(2,1)} %shard_map.125), calls=%async_computation.1 | async-start | bytes 196608 | tf_op jit(solution)/shard_map/all_to_all | solution.py:316
  43.1 19.6 %collective-permute-start.1 = (bf16[2,144,256]{2,1,0:T(8,128)(2,1)S(1)}, bf16[2,144,256]{2,1,0:T(8,128)(2,1)S(1)}, u32[]{:S(2)}, u32[]{:S(2)}) collective-permute-start(bf16[2,144,256]{2,1,0:T(8,128)(2,1)S(1)} %get-tuple-element.24.rest_0_), channel_id=1, source_target_pairs={{0,4},{1,5},{2,6},{3,7},{4,0},{5,1},{6,2},{7,3},{8,12},{9,13},{10,... | collective-permute-start | bytes 442376 | tf_op jit(solution)/shard_map/ppermute | solution.py:320
  49.4 21.7 %all-to-all-start.2 = ((bf16[64,8,128]{2,1,0:T(8,128)(2,1)}), bf16[64,8,128]{2,1,0:T(8,128)(2,1)S(1)}, u32[]{:S(2)}, u32[]{:S(2)}) async-start(bf16[64,8,128]{2,1,0:T(8,128)(2,1)} %shard_map.128), calls=%async_computation.2 | async-start | bytes 262144 | tf_op jit(solution)/shard_map/all_to_all | solution.py:316
  62.7 7.6 %collective-permute-start.2 = (bf16[144,256]{1,0:T(8,128)(2,1)S(1)}, bf16[144,256]{1,0:T(8,128)(2,1)S(1)}, u32[]{:S(2)}, u32[]{:S(2)}) collective-permute-start(bf16[144,256]{1,0:T(8,128)(2,1)S(1)} %get-tuple-element.27.rest_2_), channel_id=1, source_target_pairs={{0,1},{1,0},{2,3},{3,2},{4,5},{5,4},{6,7},{7,6},{8,9},{9,8},{10,11... | collective-permute-start | bytes 221192 | tf_op jit(solution)/shard_map/ppermute | solution.py:320

commit v5 on v4

--- a/solution.py
+++ b/solution.py
@@ -232,8 +232,10 @@
     )
 
 
-def combine_kernel(message_ref, owner_ref, out_ref, stat_ref, fresh_ref, kv_ref, final_ref, new_kv_ref):
+def combine_kernel(message_ref, owner_ref, out_ref, stat_ref, fresh_ref, kv_ref, final_hbm, new_kv_hbm, final_ref, sems):
     heads, requests, width = out_ref.shape
+    stores = [pltpu.make_async_copy(kv_ref, new_kv_hbm, sems.at[heads])]
+    stores[0].start()
     messages = jnp.swapaxes(message_ref[...].astype(F32), 0, 1)
     levels = messages[heads]
     levels = levels[:, :SLOTS] + levels[:, SLOTS : 2 * SLOTS] + levels[:, 2 * SLOTS : 3 * SLOTS]
@@ -254,7 +256,6 @@
     columns = jnp.concatenate(
         [factor * inverse, fresh * inverse, jnp.zeros((LANES - 2 * SLOTS, requests), F32)], axis=0
     ).T
-    new_kv_ref[...] = kv_ref[...]
     value = kv_ref[:, width:].astype(F32)
     for h in range(heads):
         weight = weights[h] * inverse[h : h + 1]
@@ -268,15 +269,20 @@
             preferred_element_type=F32,
         )
         total = total + out_ref[h] * columns[:, h : h + 1] + value * columns[:, SLOTS + h : SLOTS + h + 1]
+        lanes = pl.ds(h * width, width)
         final_ref[:, h * width : (h + 1) * width] = total.astype(BF16)
-
-
-def call(kernel, shapes, ins, scratch=(), limit=8, flops=10**9, moved=0):
+        stores.append(pltpu.make_async_copy(final_ref.at[:, lanes], final_hbm.at[:, lanes], sems.at[h]))
+        stores[-1].start()
+    for store in stores:
+        store.wait()
+
+
+def call(kernel, shapes, ins, scratch=(), limit=8, flops=10**9, moved=0, outs=VMEM):
     return pl.pallas_call(
         kernel,
         out_shape=shapes,
         in_specs=ins,
-        out_specs=jax.tree.map(lambda _: VMEM, shapes),
+        out_specs=jax.tree.map(lambda _: outs, shapes),
         scratch_shapes=scratch,
         compiler_params=pltpu.CompilerParams(vmem_limit_bytes=limit * 1024 * 1024),
         cost_estimate=pl.CostEstimate(flops=flops, bytes_accessed=moved, transcendentals=0),
@@ -405,6 +411,8 @@
         combine_kernel,
         [shape((requests, heads * width), BF16), shape((requests, 2 * width), BF16)],
         [VMEM] * 6,
+        [pltpu.VMEM((requests, heads * width), BF16), pltpu.SemaphoreType.DMA((heads + 1,))],
+        outs=ANY,
     )(answers, owner, out, stats, fresh, kv)
     return (attention_out, new_kv.reshape(requests, 1, 2 * width))
 

time: 72.9 us -> 72.9 us (level)
  no operation moved by 1% of the time
where the time goes in v5:
time: 72.9 us; the launch traced here: 72.5 us
  starting transfers between devices  59.1 us (81%)
  Pallas kernels  9.28 us (13%)
  waiting for transfers between devices  1.5 us (2%)
  between operations  0.87 us (1%)
  other arithmetic  0.82 us (1%)
    all_to_all x3, starting transfers between devices, exchange(): lax.all_to_all(x, 'inst', 0, 0, tiled=True, axis_index_groups=[order])  46.8 us
    ppermute x3, starting transfers between devices, swap(): return lax.ppermute(x, 'tp', [(i, i ^ bit) for i in range(ranks)])  12.3 us
    pallas_call x2, Pallas kernels, local(): call(functools.partial(local_kernel, scale, first), [shape((stop, request...  4.09 us
  transfers between devices with their start and end apart: 6, of which 3 were waited for; matrix products, arithmetic and copies ran while one was open for 1% of the time, Pallas kernels for 10%

profile of v5, /device:TPU:1, one launch (start us, length us, event | category | flops | bytes accessed | tf_op | source)
XLA Modules:
  0.0 72.5 jit_solution(5310903178411595543)
XLA Ops:
  0.6 0.7 fusion.8.plan_ref
  1.3 0.7 %shard_map.122 = s32[64,1,128]{2,1,0:T(1,128)} custom-call(s32[1,32]{1,0:T(1,128)S(1)} %fusion.8.plan_ref), custom_call_target="tpu_custom_call" | custom-call | flops 10000000000 | tf_op jit(solution)/shard_map/pallas_call | solution.py:334
  2.1 19.9 %all-to-all-start = ((s32[64,1,128]{2,1,0:T(1,128)}), s32[64,1,128]{2,1,0:T(1,128)S(1)}, u32[]{:S(2)}, u32[]{:S(2)}) async-start(s32[64,1,128]{2,1,0:T(1,128)} %shard_map.122), calls=%async_computation | async-start | bytes 65536 | tf_op jit(solution)/shard_map/all_to_all | solution.py:322
  22.0 0.2 shard_map.123
  22.2 0.7 fusion.2.partial_ref
  22.8 0.0 copy-start.1
  22.8 0.0 copy-start.2
  22.9 0.0 copy-start.4
  22.9 0.0 copy-start.5
  22.9 0.1 shard_map.124
  23.0 3.2 %collective-permute-start = (bf16[2,2,144,256]{3,2,1,0:T(8,128)(2,1)S(1)}, bf16[2,2,144,256]{3,2,1,0:T(8,128)(2,1)S(1)}, u32[]{:S(2)}, u32[]{:S(2)}) collective-permute-start(bf16[2,2,144,256]{3,2,1,0:T(8,128)(2,1)S(1)} %get-tuple-element.21.rest_0_), channel_id=1, source_target_pairs={{0,2},{1,3},{2,0},{3,1},{4,6},{5,7},{6,4},{7,5},{8,10},{9,11},{10,... | collective-permute-start | bytes 884744 | tf_op jit(solution)/shard_map/ppermute | solution.py:326
  26.2 0.0 all-to-all-done.label_ref
  26.2 0.9 %shard_map.125 = bf16[64,2,384]{2,1,0:T(2,128)(2,1)} custom-call(s32[64,1,128]{2,1,0:T(1,128)S(1)} %all-to-all-done.label_ref, bf16[6,128,128]{2,1,0:T(8,128)(2,1)S(1)} %bitcast.27, bf16[2,2,144,256]{3,2,1,0:T(8,128)(2,1)S(1)} %get-tuple-element.21.rest_0_), custom_call_target="tpu_custom_call" | custom-call | flops 1000000000 | tf_op jit(solution)/shard_map/pallas_call | solution.py:366
  27.1 13.8 %all-to-all-start.1 = ((bf16[64,2,384]{2,1,0:T(2,128)(2,1)}), bf16[64,2,384]{2,1,0:T(2,128)(2,1)S(1)}, u32[]{:S(2)}, u32[]{:S(2)}) async-start(bf16[64,2,384]{2,1,0:T(2,128)(2,1)} %shard_map.125), calls=%async_computation.1 | async-start | bytes 196608 | tf_op jit(solution)/shard_map/all_to_all | solution.py:322
  40.9 0.0 copy-done.1
  40.9 2.0 %shard_map.126 = (f32[3,128,128]{2,1,0:T(8,128)S(1)}, f32[16,128]{1,0:T(8,128)S(1)}) custom-call(bf16[6,128,128]{2,1,0:T(8,128)(2,1)S(1)} %bitcast.28, bf16[20,128,128]{2,1,0:T(8,128)(2,1)S(1)} %bitcast.21, bf16[20,128,128]{2,1,0:T(8,128)(2,1)S(1)} %bitcast.24, s32[12,128]{1,0:T(8,128)S(1)} %bitcast.31, s32[1,128]{1,0:T(1,128)S(1)} %bitcast.33), custom_call_target="tpu_custom_call" | custom-call | flops 3000000000 | tf_op jit(solution)/shard_map/pallas_call | solution.py:357
  43.0 0.0 collective-permute-done.got_ref
  43.0 0.1 shard_map.127
  43.1 4.3 %collective-permute-start.1 = (bf16[2,144,256]{2,1,0:T(8,128)(2,1)S(1)}, bf16[2,144,256]{2,1,0:T(8,128)(2,1)S(1)}, u32[]{:S(2)}, u32[]{:S(2)}) collective-permute-start(bf16[2,144,256]{2,1,0:T(8,128)(2,1)S(1)} %get-tuple-element.24.rest_0_), channel_id=1, source_target_pairs={{0,4},{1,5},{2,6},{3,7},{4,0},{5,1},{6,2},{7,3},{8,12},{9,13},{10,... | collective-permute-start | bytes 442376 | tf_op jit(solution)/shard_map/ppermute | solution.py:326
  47.5 0.6 all-to-all-done.1.asked_ref
  48.1 1.4 %shard_map.128 = bf16[64,8,128]{2,1,0:T(8,128)(2,1)} custom-call(s32[1,32]{1,0:T(1,128)S(1)} %fusion.8.plan_ref, bf16[64,2,384]{2,1,0:T(2,128)(2,1)S(1)} %all-to-all-done.1.asked_ref, bf16[20,128,128]{2,1,0:T(8,128)(2,1)S(1)} %bitcast.22, bf16[20,128,128]{2,1,0:T(8,128)(2,1)S(1)} %bitcast.25, bf16[2,144,256]{2,1,0:T(8,128)(2,1)S(1)} %get-tuple-element.24.rest_0_), custom_call_target="tpu_custom_call" | custom-call | flops 1000000000 | tf_op jit(solution)/shard_map/pallas_call | solution.py:378
  49.4 13.2 %all-to-all-start.2 = ((bf16[64,8,128]{2,1,0:T(8,128)(2,1)}), bf16[64,8,128]{2,1,0:T(8,128)(2,1)S(1)}, u32[]{:S(2)}, u32[]{:S(2)}) async-start(bf16[64,8,128]{2,1,0:T(8,128)(2,1)} %shard_map.128), calls=%async_computation.2 | async-start | bytes 262144 | tf_op jit(solution)/shard_map/all_to_all | solution.py:322
  62.6 0.0 collective-permute-done.1.got_ref
  62.6 0.1 shard_map.130
  62.7 4.7 %collective-permute-start.2 = (bf16[144,256]{1,0:T(8,128)(2,1)S(1)}, bf16[144,256]{1,0:T(8,128)(2,1)S(1)}, u32[]{:S(2)}, u32[]{:S(2)}) collective-permute-start(bf16[144,256]{1,0:T(8,128)(2,1)S(1)} %get-tuple-element.27.rest_2_), channel_id=1, source_target_pairs={{0,1},{1,0},{2,3},{3,2},{4,5},{5,4},{6,7},{7,6},{8,9},{9,8},{10,11... | collective-permute-start | bytes 221192 | tf_op jit(solution)/shard_map/ppermute | solution.py:326
  67.5 0.2 fusion.9
  67.7 2.0 %shard_map.131 = (f32[6,128,128]{2,1,0:T(8,128)S(1)}, f32[16,128]{1,0:T(8,128)S(1)}) custom-call(bf16[6,128,128]{2,1,0:T(8,128)(2,1)S(1)} %bitcast.29, bf16[20,128,128]{2,1,0:T(8,128)(2,1)S(1)} %bitcast.23, bf16[20,128,128]{2,1,0:T(8,128)(2,1)S(1)} %bitcast.26, s32[12,128]{1,0:T(8,128)S(1)} %bitcast.32, s32[1,128]{1,0:T(1,128)S(1)} %bitcast.35, ...), custom_call_target="tpu_custom_call" | custom-call | flops 200000000 | tf_op jit(solution)/shard_map/pallas_call | solution.py:357
  69.8 0.1 pad_maximum_fusion
  69.9 0.5 collective-permute-done.2.got_ref
  70.4 0.4 shard_map.132
  70.8 0.4 all-to-all-done.2.message_ref
  71.2 1.4 %shard_map.133 = (bf16[128,768]{1,0:T(8,128)(2,1)}, bf16[128,256]{1,0:T(8,128)(2,1)}) custom-call(bf16[64,8,128]{2,1,0:T(8,128)(2,1)S(1)} %all-to-all-done.2.message_ref, f32[64,128]{1,0:T(8,128)S(1)} %shard_map.129.owner_ref, f32[6,128,128]{2,1,0:T(8,128)S(1)} %get-tuple-element.28.out_ref, f32[16,128]{1,0:T(8,128)S(1)} %get-tuple-element.29.stat_ref, ...), custom_call_target="tpu_custom_call" | custom-call | flops 1000000000 | tf_op jit(solution)/shard_map/pallas_call | solution.py:410
  (14 shorter events, 0.1 us)
Async XLA Ops:
  1.3 20.6 %copy-start = (bf16[768,8,256]{2,1,0:T(8,128)(2,1)S(1)}, bf16[768,8,256]{2,1,0:T(8,128)(2,1)}, u32[]{:S(2)}) copy-start(bf16[768,8,256]{2,1,0:T(8,128)(2,1)} %_.1) | copy-start | bytes 9437188
  1.3 20.7 %copy-start.6 = (bf16[128,768]{1,0:T(8,128)(2,1)S(1)}, bf16[128,768]{1,0:T(8,128)(2,1)}, u32[]{:S(2)}) copy-start(bf16[128,768]{1,0:T(8,128)(2,1)} %hidden_ref.1) | copy-start | bytes 589828
  1.3 20.7 %copy-start.7 = (bf16[768]{0:T(1024)(128)(2,1)S(1)}, bf16[768]{0:T(1024)(128)(2,1)}, u32[]{:S(2)}) copy-start(bf16[768]{0:T(1024)(128)(2,1)} %gain_ref.1) | copy-start | bytes 4612
  2.1 24.1 %all-to-all-start = ((s32[64,1,128]{2,1,0:T(1,128)}), s32[64,1,128]{2,1,0:T(1,128)S(1)}, u32[]{:S(2)}, u32[]{:S(2)}) async-start(s32[64,1,128]{2,1,0:T(1,128)} %shard_map.122), calls=%async_computation | async-start | bytes 65536 | tf_op jit(solution)/shard_map/all_to_all | solution.py:322
  22.2 4.1 %copy-start.3 = (bf16[128,6,128]{2,0,1:T(8,128)(2,1)S(1)}, bf16[128,6,128]{2,0,1:T(8,128)(2,1)}, u32[]{:S(2)}) copy-start(bf16[128,6,128]{2,0,1:T(8,128)(2,1)} %param.14) | copy-start | bytes 589828
  22.8 18.1 %copy-start.1 = (bf16[20,1,128,128]{3,2,1,0:T(8,128)(2,1)S(1)}, bf16[20,1,128,128]{3,2,1,0:T(8,128)(2,1)}, u32[]{:S(2)}) copy-start(bf16[20,1,128,128]{3,2,1,0:T(8,128)(2,1)} %param.15) | copy-start | bytes 1966084
  22.8 18.1 %copy-start.2 = (bf16[20,1,128,128]{3,2,1,0:T(8,128)(2,1)S(1)}, bf16[20,1,128,128]{3,2,1,0:T(8,128)(2,1)}, u32[]{:S(2)}) copy-start(bf16[20,1,128,128]{3,2,1,0:T(8,128)(2,1)} %param.16) | copy-start | bytes 1966084
  22.9 18.1 %copy-start.4 = (s32[128,12]{0,1:T(8,128)S(1)}, s32[128,12]{0,1:T(8,128)}, u32[]{:S(2)}) copy-start(s32[128,12]{0,1:T(8,128)} %param.17) | copy-start | bytes 18436
  22.9 18.1 %copy-start.5 = (s32[128]{0:T(128)S(1)}, s32[128]{0:T(128)}, u32[]{:S(2)}) copy-start(s32[128]{0:T(128)} %param.18) | copy-start | bytes 1540
  23.0 20.0 %collective-permute-start = (bf16[2,2,144,256]{3,2,1,0:T(8,128)(2,1)S(1)}, bf16[2,2,144,256]{3,2,1,0:T(8,128)(2,1)S(1)}, u32[]{:S(2)}, u32[]{:S(2)}) collective-permute-start(bf16[2,2,144,256]{3,2,1,0:T(8,128)(2,1)S(1)} %get-tuple-element.21.rest_0_), channel_id=1, source_target_pairs={{0,2},{1,3},{2,0},{3,1},{4,6},{5,7},{6,4},{7,5},{8,10},{9,11},{10,... | collective-permute-start | bytes 884744 | tf_op jit(solution)/shard_map/ppermute | solution.py:326
  27.1 20.9 %all-to-all-start.1 = ((bf16[64,2,384]{2,1,0:T(2,128)(2,1)}), bf16[64,2,384]{2,1,0:T(2,128)(2,1)S(1)}, u32[]{:S(2)}, u32[]{:S(2)}) async-start(bf16[64,2,384]{2,1,0:T(2,128)(2,1)} %shard_map.125), calls=%async_computation.1 | async-start | bytes 196608 | tf_op jit(solution)/shard_map/all_to_all | solution.py:322
  43.1 19.6 %collective-permute-start.1 = (bf16[2,144,256]{2,1,0:T(8,128)(2,1)S(1)}, bf16[2,144,256]{2,1,0:T(8,128)(2,1)S(1)}, u32[]{:S(2)}, u32[]{:S(2)}) collective-permute-start(bf16[2,144,256]{2,1,0:T(8,128)(2,1)S(1)} %get-tuple-element.24.rest_0_), channel_id=1, source_target_pairs={{0,4},{1,5},{2,6},{3,7},{4,0},{5,1},{6,2},{7,3},{8,12},{9,13},{10,... | collective-permute-start | bytes 442376 | tf_op jit(solution)/shard_map/ppermute | solution.py:326
  49.4 21.7 %all-to-all-start.2 = ((bf16[64,8,128]{2,1,0:T(8,128)(2,1)}), bf16[64,8,128]{2,1,0:T(8,128)(2,1)S(1)}, u32[]{:S(2)}, u32[]{:S(2)}) async-start(bf16[64,8,128]{2,1,0:T(8,128)(2,1)} %shard_map.128), calls=%async_computation.2 | async-start | bytes 262144 | tf_op jit(solution)/shard_map/all_to_all | solution.py:322
  62.7 7.6 %collective-permute-start.2 = (bf16[144,256]{1,0:T(8,128)(2,1)S(1)}, bf16[144,256]{1,0:T(8,128)(2,1)S(1)}, u32[]{:S(2)}, u32[]{:S(2)}) collective-permute-start(bf16[144,256]{1,0:T(8,128)(2,1)S(1)} %get-tuple-element.27.rest_2_), channel_id=1, source_target_pairs={{0,1},{1,0},{2,3},{3,2},{4,5},{5,4},{6,7},{7,6},{8,9},{9,8},{10,11... | collective-permute-start | bytes 221192 | tf_op jit(solution)/shard_map/ppermute | solution.py:326
